TPU v7x, 256 devices: a whole 4x4x8 slice. The times are simulated.
256 devices in a mesh: grp: 4 (over y), wide: 64 (over x, z, core).
Axes of the slice: x: 4, y: 4, z: 8, core: 2. Of those that a mesh axis runs over, the one named last changes fastest.
Arguments:
- word_table: float32 [32768, 500], P('wide'), may hold values from -1.5 to 1.5
- word_accum: float32 [32768], P('wide'), may hold values from 0.5 to 8
- ent_table: float32 [131072, 500], P(('grp', 'wide')), may hold values from -1.5 to 1.5
- ent_accum: float32 [131072], P(('grp', 'wide')), may hold values from 0.5 to 8
- anchor_word_shard: int32 [2, 32768, 1], P(None, ('grp', 'wide')), may hold values from 0 to 63; in each aligned block of 128 rows (0 to 127, 128 to 255, ..., all dimensions but the last counted through in order) at most 4 rows name the same one
- anchor_word_row: int32 [2, 32768], P(None, ('grp', 'wide')), may hold values from 0 to 511
- anchor_ent_row: int32 [2, 32768], P(None, ('grp', 'wide')), may hold values from 0 to 511
- anchor_count: int32 [2, 256], P(None, ('grp', 'wide')), may hold values from 16 to 128
- link_src_row: int32 [2, 32768], P(None, ('grp', 'wide')), may hold values from 0 to 511
- link_dst_shard: int32 [2, 32768, 1], P(None, ('grp', 'wide')), may hold values from 0 to 63; in each aligned block of 128 rows (0 to 127, 128 to 255, ..., all dimensions but the last counted through in order) at most 4 rows name the same one
- link_dst_row: int32 [2, 32768], P(None, ('grp', 'wide')), may hold values from 0 to 511
- link_count: int32 [2, 256], P(None, ('grp', 'wide')), may hold values from 16 to 128
- neg_rows: int32 [2, 512, 512], P(None, ('grp', 'wide')), may hold values from 0 to 511
Outputs:
- word_new: float32 [32768, 500], P('wide')
- word_accum_new: float32 [32768], P('wide')
- ent_new: float32 [131072, 500], P(('grp', 'wide'))
- ent_accum_new: float32 [131072], P(('grp', 'wide'))
Inputs may be any that keep to these rules, and one draw needn't show every extreme that they name: `anchor_word_shard`: in each minibatch, the 128 anchor rows of one device name any one shard at most 4 times, a bound that some block reaches. `link_dst_shard`: in each minibatch, the 128 link rows of one device name any one shard at most 4 times, a bound that some block reaches.
All inputs are finite; a program needn't handle non-finite values.
Results may differ from a plain program's by a relative error of at most 0.0017.
Values may be sent and summed in bfloat16 or wider, within the bound.
No kernel may reach another device: no remote copies, remote signals or barrier semaphores. Data moves between devices by JAX's collectives and lax.ppermute only.
A program may use at most 64 MiB of HBM per device.

v0:
```python
import functools

import jax
import jax.numpy as jnp
from jax import lax
from jax.experimental import pallas as pl
from jax.experimental.pallas import tpu as pltpu
from jax.sharding import PartitionSpec as P

BLOCK = 128
STEPS = 2
LEARN = 0.1
CAP = 4
HALF = 256
CUT = 248
PAD = 2 * HALF
ID_HI = 252
ID_LO = 253
F32 = jnp.float32
BF16 = jnp.bfloat16

PLACE_W, PLACE_L, ANCHOR_ENT, LINK_SRC, RANK_W, RANK_L, WORD_ROW, LINK_ROW = range(8)


def iota(shape, dim):
    return lax.broadcasted_iota(jnp.int32, shape, dim).astype(F32)


def nn(a, b):
    return lax.dot_general(a, b, (((1,), (0,)), ((), ())), preferred_element_type=F32)


def nt(a, b):
    return lax.dot_general(a, b, (((1,), (1,)), ((), ())), preferred_element_type=F32)


def hot(condition):
    return jnp.where(condition, 1.0, 0.0).astype(BF16)


def split(x):
    high = x.astype(BF16)
    return high, (x - high.astype(F32)).astype(BF16)


def kernel_call(body, out_shape, name, scratch=(), smem=(), operands=(), flops=0, moved=0):
    in_specs = [
        pl.BlockSpec(memory_space=pltpu.SMEM if i in smem else pltpu.VMEM)
        for i in range(len(operands))
    ]
    out_specs = jax.tree.map(lambda _: pl.BlockSpec(memory_space=pltpu.VMEM), out_shape)
    return pl.pallas_call(
        body,
        out_shape=out_shape,
        in_specs=in_specs,
        out_specs=out_specs,
        scratch_shapes=list(scratch),
        name=name,
        compiler_params=pltpu.CompilerParams(vmem_limit_bytes=40 * 2**20),
        cost_estimate=pl.CostEstimate(flops=flops, bytes_accessed=moved, transcendentals=0),
    )(*operands)


def prepare_body(aws, awr, aer, lsr, lds, ldr, asks_ref, rows_ref, cols_ref, table):
    peers = asks_ref.shape[0]
    table[...] = jnp.zeros_like(table)
    earlier = hot(iota((BLOCK, BLOCK), 0) < iota((BLOCK, BLOCK), 1))
    peer = iota((peers, BLOCK), 0)
    owned = []
    for step in range(STEPS):
        for kind, (shard_ref, row_ref) in enumerate(((aws, awr), (lds, ldr))):
            shard = shard_ref[step : step + 1, :].astype(F32)
            owner = peer == shard
            before = nn(hot(owner), earlier)
            rank = jnp.sum(jnp.where(owner, before, 0.0), axis=0, keepdims=True)
            base = 8 * step
            table[base + PLACE_W + kind : base + PLACE_W + kind + 1, :] = shard * (2 * CAP) + rank
            table[base + RANK_W + kind : base + RANK_W + kind + 1, :] = rank
            table[base + WORD_ROW + kind : base + WORD_ROW + kind + 1, :] = row_ref[
                step : step + 1, :
            ].astype(F32)
            owned.append(hot(owner))
        table[8 * step + ANCHOR_ENT : 8 * step + ANCHOR_ENT + 1, :] = aer[
            step : step + 1, :
        ].astype(F32)
        table[8 * step + LINK_SRC : 8 * step + LINK_SRC + 1, :] = lsr[step : step + 1, :].astype(
            F32
        )
    rows_ref[...] = table[0:16, :]
    cols = jnp.transpose(table[...])
    cols_ref[...] = cols
    lane = iota((BLOCK, BLOCK), 1)
    asks = jnp.zeros((peers, BLOCK), F32)
    for step in range(STEPS):
        for kind in range(2):
            rank = cols[:, 8 * step + RANK_W + kind : 8 * step + RANK_W + kind + 1]
            row = cols[:, 8 * step + WORD_ROW + kind : 8 * step + WORD_ROW + kind + 1]
            high = jnp.floor(row * (1.0 / 16.0))
            place = (2 * step + kind) * CAP + rank
            value = jnp.where(lane == place, high, jnp.where(lane == place + 64.0, row - 16.0 * high, 0.0))
            asks = asks + nn(owned[2 * step + kind], value.astype(BF16))
    asks_ref[...] = asks.astype(jnp.int32)


def to_half(ref, out_ref, scratch):
    scratch[CUT:HALF, :] = jnp.zeros((HALF - CUT, scratch.shape[1]), F32)
    scratch[PAD - 8 : PAD, :] = jnp.zeros((8, scratch.shape[1]), F32)
    scratch[0:CUT, :] = ref[0:CUT, :]
    scratch[HALF : HALF + ref.shape[0] - CUT, :] = ref[CUT:, :]
    out_ref[...] = scratch[...].astype(BF16)


def halves_body(ent_ref, word_ref, neg_ref, ent_out, word_out, counts_out, scratch):
    to_half(ent_ref, ent_out, scratch)
    to_half(word_ref, word_out, scratch)
    entity = iota((ent_ref.shape[1], neg_ref.shape[1]), 0)
    ones = jnp.ones((8, neg_ref.shape[1]), BF16)
    for i in range(2 * STEPS):
        named = hot(entity == neg_ref[i : i + 1, :].astype(F32))
        counts_out[8 * i : 8 * i + 8, :] = nt(ones, named)


def id_column(asks_ref, which):
    peers = asks_ref.shape[0]
    rows = peers * 2 * CAP
    source = hot(
        lax.broadcasted_iota(jnp.int32, (rows, peers), 0) // (2 * CAP)
        == lax.broadcasted_iota(jnp.int32, (rows, peers), 1)
    )
    spread = nn(source, asks_ref[...].astype(BF16))
    lane = lax.broadcasted_iota(jnp.int32, (rows, BLOCK), 1)
    place = which * CAP + lax.broadcasted_iota(jnp.int32, (rows, BLOCK), 0) % CAP
    weight = jnp.where(lane == place, 16.0, jnp.where(lane == place + 64, 1.0, 0.0))
    return jnp.sum(spread * weight, axis=1, keepdims=True)


def first_half(rows):
    return lax.broadcasted_iota(jnp.int32, (rows, HALF), 0) % (2 * CAP) < CAP


def answer(asks_ref, which, half_ref):
    ids = id_column(asks_ref, which)
    rows = ids.shape[0]
    named = hot(iota((rows, half_ref.shape[1]), 1) == ids)
    low = nt(named, half_ref[0:HALF, :])
    high = nt(named, half_ref[HALF:PAD, :])
    return jnp.where(first_half(rows), low, high).astype(BF16)


def respond_body(step, asks_ref, word_half, ent_half, out_ref):
    out_ref[:, 0:HALF] = answer(asks_ref, 2 * step, word_half)
    out_ref[:, HALF:PAD] = answer(asks_ref, 2 * step + 1, ent_half)


def column(cols_ref, step, which):
    return cols_ref[:, 8 * step + which : 8 * step + which + 1]


def valid(count):
    return jnp.where(lax.broadcasted_iota(jnp.int32, (BLOCK, 1), 0) < count, 1.0, 0.0)


def sigmoid(x):
    return jax.nn.sigmoid(x)


def link_local_body(step, link_count, cols_ref, counts_ref, ent_half, src_out, coef_out, grad_out):
    entities = ent_half.shape[1]
    mask = valid(link_count[step])
    source = hot(iota((BLOCK, entities), 1) == column(cols_ref, step, LINK_SRC))
    src = nt(source, ent_half[...]).astype(BF16)
    src_out[...] = src
    push = (mask * sigmoid(nn(src, ent_half[...]))).astype(BF16).astype(F32)
    count = counts_ref[16 * step + 8 : 16 * step + 9, :]
    coef = push * count
    coef_out[...] = coef
    high, low = split(coef)
    grad_out[...] = nt(high, ent_half[...]) + nt(low, ent_half[...])


def take(recv, place):
    rows = recv.shape[0]
    lane = iota((BLOCK, rows), 1)
    return jnp.concatenate([nn(hot(lane == place), recv), nn(hot(lane == place + CAP), recv)], axis=1)


def put(place, low, high, rows):
    row = iota((rows, BLOCK), 0)
    return nn(hot(row == place), low) + nn(hot(row == place + CAP), high)


def blocks_body(
    step,
    anchor_count,
    link_count,
    recv_ref,
    rows_ref,
    cols_ref,
    counts_ref,
    ent_half,
    src_ref,
    link_grad_ref,
    send_ref,
    words_out,
    coef_out,
    link_out,
):
    entities = ent_half.shape[1]
    message_rows = recv_ref.shape[0]
    words = take(recv_ref[:, 0:HALF], column(cols_ref, step, PLACE_W)).astype(BF16)
    words_out[...] = words
    mask = valid(anchor_count[step])
    score = nn(words, ent_half[...])
    target = iota((BLOCK, entities), 1) == column(cols_ref, step, ANCHOR_ENT)
    pos = jnp.sum(jnp.where(target, score, 0.0), axis=1, keepdims=True)
    pull = mask * (sigmoid(pos) - 1.0)
    push = (mask * sigmoid(score)).astype(BF16).astype(F32)
    count = counts_ref[16 * step : 16 * step + 1, :]
    coef = push * count + jnp.where(target, pull, 0.0)
    coef_out[...] = coef
    high, low = split(coef)
    centre = nt(high, ent_half[...]) + nt(low, ent_half[...])
    word_row = column(cols_ref, step, WORD_ROW)
    id_high = jnp.floor(word_row * (1.0 / 16.0))
    lane = lax.broadcasted_iota(jnp.int32, (BLOCK, PAD), 1) % HALF
    centre = jnp.where(lane == ID_HI, id_high, jnp.where(lane == ID_LO, word_row - 16.0 * id_high, centre))
    centre = centre.astype(BF16)
    place = rows_ref[8 * step + PLACE_W : 8 * step + PLACE_W + 1, :]
    send_ref[:, 0:HALF] = put(place, centre[:, 0:HALF], centre[:, HALF:PAD], message_rows).astype(BF16)

    targets = take(recv_ref[:, HALF:PAD], column(cols_ref, step, PLACE_L))
    src = src_ref[...].astype(F32)
    pos = jnp.sum(src * targets, axis=1, keepdims=True)
    pull = valid(link_count[step]) * (sigmoid(pos) - 1.0)
    link_out[...] = pull * targets + link_grad_ref[...]
    grad = (pull * src).astype(BF16)
    place = rows_ref[8 * step + PLACE_L : 8 * step + PLACE_L + 1, :]
    send_ref[:, HALF:PAD] = put(place, grad[:, 0:HALF], grad[:, HALF:PAD], message_rows).astype(BF16)


def ent_local_body(step, words_ref, coef_ref, src_ref, link_coef_ref, link_ref, cols_ref, out_ref):
    entities = out_ref.shape[1]
    words = jnp.transpose(words_ref[...].astype(F32)).astype(BF16)
    high, low = split(coef_ref[...])
    total = nn(words, high) + nn(words, low)
    src = jnp.transpose(src_ref[...].astype(F32)).astype(BF16)
    high, low = split(link_coef_ref[...])
    total = total + nn(src, high) + nn(src, low)
    source = hot(iota((BLOCK, entities), 1) == column(cols_ref, step, LINK_SRC))
    high, low = split(jnp.transpose(link_ref[...]))
    out_ref[...] = total + nn(high, source) + nn(low, source)


def adagrad(table_ref, accum_ref, low, high, table_out, accum_out):
    width = table_ref.shape[0]
    low = low[0:CUT, :]
    high = high[0 : width - CUT, :]
    square = jnp.sum(low * low, axis=0, keepdims=True) + jnp.sum(high * high, axis=0, keepdims=True)
    accum = accum_ref[...] + square * (1.0 / width)
    accum_out[...] = accum
    rate = LEARN * lax.rsqrt(accum)
    table_out[0:CUT, :] = table_ref[0:CUT, :] - low * rate
    table_out[CUT:, :] = table_ref[CUT:, :] - high * rate


def ent_update_body(
    step, last, asks_ref, recv_ref, local_ref, table_ref, accum_ref, table_out, accum_out, *rest
):
    rows = recv_ref.shape[0]
    named = hot(iota((rows, local_ref.shape[1]), 1) == id_column(asks_ref, 2 * step + 1))
    grads = jnp.transpose(recv_ref[:, HALF:PAD].astype(F32))
    lower = lax.broadcasted_iota(jnp.int32, grads.shape, 1) % (2 * CAP) < CAP
    low = nn(jnp.where(lower, grads, 0.0).astype(BF16), named) + local_ref[0:HALF, :]
    high = nn(jnp.where(lower, 0.0, grads).astype(BF16), named) + local_ref[HALF:PAD, :]
    adagrad(table_ref, accum_ref, low, high, table_out, accum_out)
    if not last:
        half_out, scratch = rest
        to_half(table_out, half_out, scratch)


def word_update_body(step, last, recv_ref, table_ref, accum_ref, *rest):
    if last:
        table_out, accum_out = rest
    else:
        asks_ref, ent_half, table_out, accum_out, send_ref, half, scratch = rest
    words = table_ref.shape[1]
    part = 512
    low = jnp.zeros((HALF, words), F32)
    high = jnp.zeros((HALF, words), F32)
    for start in range(0, recv_ref.shape[0], part):
        grads = recv_ref[start : start + part, :].astype(F32)
        lane = lax.broadcasted_iota(jnp.int32, (part, HALF), 1)
        weight = jnp.where(lane == ID_HI, 16.0, jnp.where(lane == ID_LO, 1.0, 0.0))
        ids = jnp.sum(grads * weight, axis=1, keepdims=True)
        named = hot(iota((part, words), 1) == ids)
        grads = jnp.transpose(grads)
        lower = lax.broadcasted_iota(jnp.int32, grads.shape, 1) % (2 * CAP) < CAP
        low = low + nn(jnp.where(lower, grads, 0.0).astype(BF16), named)
        high = high + nn(jnp.where(lower, 0.0, grads).astype(BF16), named)
    adagrad(table_ref, accum_ref, low, high, table_out, accum_out)
    if not last:
        to_half(table_out, half, scratch)
        respond_body(step + 1, asks_ref, half, ent_half, send_ref)


def shape(*dims, dtype=F32):
    return jax.ShapeDtypeStruct(dims, dtype)


def exchange(x, axis, groups):
    return lax.all_to_all(x, axis, split_axis=0, concat_axis=0, tiled=True)


def on_device(
    word_table,
    word_accum,
    ent_table,
    ent_accum,
    anchor_word_shard,
    anchor_word_row,
    anchor_ent_row,
    anchor_count,
    link_src_row,
    link_dst_shard,
    link_dst_row,
    link_count,
    neg_rows,
):
    peers = lax.axis_size("wide")
    groups = lax.axis_size("grp")
    message = peers * 2 * CAP
    word, ent = word_table.T, ent_table.T
    word_sum, ent_sum = word_accum[None, :], ent_accum[None, :]
    width, words = word.shape
    entities = ent.shape[1]
    anchor_count, link_count = anchor_count[:, 0], link_count[:, 0]
    table_scratch = pltpu.VMEM((PAD, entities), F32)

    asks, rows, cols = kernel_call(
        prepare_body,
        (shape(peers, BLOCK, dtype=jnp.int32), shape(16, BLOCK), shape(BLOCK, BLOCK)),
        "prepare",
        scratch=(pltpu.VMEM((BLOCK, BLOCK), F32),),
        operands=(
            anchor_word_shard[:, :, 0],
            anchor_word_row,
            anchor_ent_row,
            link_src_row,
            link_dst_shard[:, :, 0],
            link_dst_row,
        ),
        moved=2**18,
    )
    asked = exchange(asks[:, None, :], "wide", None)[:, 0, :]
    ent_half, word_half, counts = kernel_call(
        halves_body,
        (
            shape(PAD, entities, dtype=BF16),
            shape(PAD, words, dtype=BF16),
            shape(8 * 2 * STEPS, entities),
        ),
        "halves",
        scratch=(table_scratch,),
        operands=(ent, word, neg_rows.reshape(-1, neg_rows.shape[-1])),
        moved=2**23,
    )
    send = kernel_call(
        functools.partial(respond_body, 0),
        shape(message, PAD, dtype=BF16),
        "respond",
        operands=(asked, word_half, ent_half),
        moved=2**22,
    )
    for step in range(STEPS):
        last = step == STEPS - 1
        recv = exchange(send, "wide", None)
        src, link_coef, link_part = kernel_call(
            functools.partial(link_local_body, step),
            (shape(BLOCK, PAD, dtype=BF16), shape(BLOCK, entities), shape(BLOCK, PAD)),
            "link_local",
            smem=(0,),
            operands=(link_count, cols, counts, ent_half),
            moved=2**22,
        )
        grads, anchor_words, anchor_coef, link_grad = kernel_call(
            functools.partial(blocks_body, step),
            (
                shape(message, PAD, dtype=BF16),
                shape(BLOCK, PAD, dtype=BF16),
                shape(BLOCK, entities),
                shape(BLOCK, PAD),
            ),
            "blocks",
            smem=(0, 1),
            operands=(anchor_count, link_count, recv, rows, cols, counts, ent_half, src, link_part),
            moved=2**22,
        )
        received = exchange(grads, "wide", None)
        local = kernel_call(
            functools.partial(ent_local_body, step),
            shape(PAD, entities),
            "ent_local",
            operands=(anchor_words, anchor_coef, src, link_coef, link_grad, cols),
            moved=2**22,
        )
        mine = jnp.broadcast_to(received[None, :, 0:HALF], (groups, message, HALF))
        every = exchange(mine.reshape(groups * message, HALF), "grp", None)
        out = kernel_call(
            functools.partial(ent_update_body, step, last),
            (shape(width, entities), shape(1, entities))
            + (() if last else (shape(PAD, entities, dtype=BF16),)),
            "ent_update",
            scratch=() if last else (table_scratch,),
            operands=(asked, received, local, ent, ent_sum),
            moved=2**22,
        )
        ent, ent_sum = out[0], out[1]
        if last:
            word, word_sum = kernel_call(
                functools.partial(word_update_body, step, True),
                (shape(width, words), shape(1, words)),
                "word_update",
                operands=(every, word, word_sum),
                moved=2**23,
            )
        else:
            ent_half = out[2]
            word, word_sum, send = kernel_call(
                functools.partial(word_update_body, step, False),
                (shape(width, words), shape(1, words), shape(message, PAD, dtype=BF16)),
                "word_update",
                scratch=(pltpu.VMEM((PAD, words), BF16), pltpu.VMEM((PAD, words), F32)),
                operands=(every, word, word_sum, asked, ent_half),
                moved=2**23,
            )
    return (word.T, word_sum[0], ent.T, ent_sum[0])


def solution(mesh):
    in_specs = (
        P("wide", None),
        P("wide"),
        P(("grp", "wide"), None),
        P(("grp", "wide")),
        P(None, ("grp", "wide"), None),
        P(None, ("grp", "wide")),
        P(None, ("grp", "wide")),
        P(None, ("grp", "wide")),
        P(None, ("grp", "wide")),
        P(None, ("grp", "wide"), None),
        P(None, ("grp", "wide")),
        P(None, ("grp", "wide")),
        P(None, ("grp", "wide"), None),
    )
    out_specs = (P("wide", None), P("wide"), P(("grp", "wide"), None), P(("grp", "wide")))
    return jax.shard_map(
        on_device, mesh=mesh, in_specs=in_specs, out_specs=out_specs, check_vma=False
    )
```

profile of v0, /device:TPU:1, one launch (start us, length us, event | category | flops | bytes accessed | tf_op | source)
XLA Modules:
  0.0 174.3 jit_solution(4627284314836416518)
XLA Ops:
  0.6 0.0 copy-start.13
  0.6 0.0 copy-start.14
  0.7 0.0 copy-start.12
  0.7 0.7 copy-done.13
  1.3 0.0 copy-done.14
  1.3 0.0 copy-done.12
  1.3 0.0 copy-start.15
  1.3 0.7 copy-done.15
  2.0 0.0 copy-start.16
  2.0 0.7 copy-done.16
  2.7 0.0 copy-start.17
  2.7 0.7 copy-done.17
  3.4 1.4 prepare.1
  4.8 0.0 copy-start.18
  4.8 13.1 %all-to-all-start = ((s32[64,1,128]{2,1,0:T(1,128)}), s32[64,1,128]{2,1,0:T(1,128)S(1)}, u32[]{:S(2)}, u32[]{:S(2)}) async-start(s32[64,1,128]{2,1,0:T(1,128)} %bitcast.5), calls=%async_computation | async-start | bytes 65536 | tf_op jit(solution)/shard_map/all_to_all | solution.py:311
  17.9 0.0 copy-done.18
  17.9 0.0 copy-start
  17.9 1.2 copy-done
  19.1 0.0 copy-start.2
  19.1 1.2 copy-done.2
  20.4 0.8 halves.1
  21.1 6.0 %all-to-all-done = s32[64,1,128]{2,1,0:T(1,128)S(1)} async-done(((s32[64,1,128]{2,1,0:T(1,128)}), s32[64,1,128]{2,1,0:T(1,128)S(1)}, u32[]{:S(2)}, u32[]{:S(2)}) %all-to-all-start) | async-done | bytes 32800 | tf_op jit(solution)/shard_map/all_to_all | solution.py:311
  27.1 1.9 %respond.1 = bf16[512,512]{1,0:T(8,128)(2,1)} custom-call(s32[64,128]{1,0:T(8,128)S(1)} %bitcast.38, bf16[512,512]{1,0:T(8,128)(2,1)S(1)} %get-tuple-element.35.word_half, bf16[512,512]{1,0:T(8,128)(2,1)S(1)} %get-tuple-element.36.ent_half), custom_call_target="tpu_custom_call" | custom-call | bytes 4194304 | tf_op jit(solution)/shard_map/respond/pallas_call | solution.py:52
  29.0 4.7 %all-to-all-start.1 = ((bf16[64,8,512]{2,1,0:T(8,128)(2,1)}), bf16[64,8,512]{2,1,0:T(8,128)(2,1)S(1)}, u32[]{:S(2)}, u32[]{:S(2)}) async-start(bf16[64,8,512]{2,1,0:T(8,128)(2,1)} %bitcast.9), calls=%async_computation.1 | async-start | bytes 1048576 | tf_op jit(solution)/shard_map/all_to_all | solution.py:311
  33.8 0.0 copy-start.8
  33.8 0.6 copy-done.8
  34.4 1.4 link_local.2
  35.8 15.3 %all-to-all-done.1 = bf16[64,8,512]{2,1,0:T(8,128)(2,1)S(1)} async-done(((bf16[64,8,512]{2,1,0:T(8,128)(2,1)}), bf16[64,8,512]{2,1,0:T(8,128)(2,1)S(1)}, u32[]{:S(2)}, u32[]{:S(2)}) %all-to-all-start.1) | async-done | bytes 524320 | tf_op jit(solution)/shard_map/all_to_all | solution.py:311
  51.1 0.0 copy-start.9
  51.1 0.7 copy-done.9
  51.8 2.0 %blocks.2 = (bf16[512,512]{1,0:T(8,128)(2,1)S(1)}, bf16[128,512]{1,0:T(8,128)(2,1)S(1)}, f32[128,512]{1,0:T(8,128)S(1)}, f32[128,512]{1,0:T(8,128)S(1)}) custom-call(s32[2]{0:T(128)S(1)} %bitcast.48, s32[2]{0:T(128)S(1)} %bitcast.45, bf16[512,512]{1,0:T(8,128)(2,1)S(1)} %bitcast.36, f32[16,128]{1,0:T(8,128)S(1)} %get-tuple-element.37.rows_ref, ...), custom_call_target="tpu_custom_call" | custom-call | bytes 4194304 | tf_op jit(solution)/shard_map/blocks/pallas_call | solution.py:52
  53.8 23.5 %all_to_all.65 = bf16[64,8,512]{2,1,0:T(8,128)(2,1)S(1)} all-to-all(bf16[64,8,512]{2,1,0:T(8,128)(2,1)S(1)} %bitcast.43), channel_id=1, replica_groups=mesh['grp'=4,'wide'=64] {'wide'}, dimensions={0} | all-to-all | bytes 1048576 | tf_op jit(solution)/shard_map/all_to_all | solution.py:311
  77.3 1.0 broadcast_in_dim.22
  78.4 4.2 %all-to-all-start.3 = ((bf16[4,512,256]{2,1,0:T(8,128)(2,1)}), bf16[4,512,256]{2,1,0:T(8,128)(2,1)S(1)}, u32[]{:S(2)}, u32[]{:S(2)}) async-start(bf16[4,512,256]{2,1,0:T(8,128)(2,1)} %broadcast_in_dim.22), calls=%async_computation.3 | async-start | bytes 2097152 | tf_op jit(solution)/shard_map/all_to_all | solution.py:311
  82.5 0.0 copy-start.1
  82.5 0.0 copy-start.10
  82.5 1.0 ent_local.2.local_ref
  83.6 0.2 copy-done.1
  83.8 0.0 copy-done.10
  83.8 0.0 copy-start.3
  83.8 1.0 ent_update.2
  84.8 0.0 copy-start.6
  84.8 1.0 copy-done.6
  85.7 11.4 %all-to-all-done.3 = bf16[4,512,256]{2,1,0:T(8,128)(2,1)S(1)} async-done(((bf16[4,512,256]{2,1,0:T(8,128)(2,1)}), bf16[4,512,256]{2,1,0:T(8,128)(2,1)S(1)}, u32[]{:S(2)}, u32[]{:S(2)}) %all-to-all-start.3) | async-done | bytes 1048608 | tf_op jit(solution)/shard_map/all_to_all | solution.py:311
  97.1 0.0 copy-done.3
  97.1 0.7 copy-done.11
  97.8 3.5 %word_update.2 = (f32[500,512]{1,0:T(8,128)S(1)}, f32[1,512]{1,0:T(1,128)S(1)}, bf16[512,512]{1,0:T(8,128)(2,1)}) custom-call(bf16[2048,256]{1,0:T(8,128)(2,1)S(1)} %bitcast.27, f32[500,512]{1,0:T(8,128)S(1)} %bitcast.31, f32[1,512]{1,0:T(1,128)S(1)} %bitcast.51, s32[64,128]{1,0:T(8,128)S(1)} %bitcast.40, bf16[512,512]{1,0:T(8,128)(2,1)S(1)} %get-tuple-element.47.rest_1_.ent_half), custom_call_target="tpu_custom_call" | custom-call | bytes 8388608 | tf_op jit(solution)/shard_map/word_update/pallas_call | solution.py:52
  101.3 0.0 copy-start.4
  101.4 1.0 copy-done.4
  102.3 7.1 %all-to-all-start.4 = ((bf16[64,8,512]{2,1,0:T(8,128)(2,1)}), bf16[64,8,512]{2,1,0:T(8,128)(2,1)S(1)}, u32[]{:S(2)}, u32[]{:S(2)}) async-start(bf16[64,8,512]{2,1,0:T(8,128)(2,1)} %bitcast.16), calls=%async_computation.4 | async-start | bytes 1048576 | tf_op jit(solution)/shard_map/all_to_all | solution.py:311
  109.4 1.4 link_local.3
  110.8 15.9 %all-to-all-done.4 = bf16[64,8,512]{2,1,0:T(8,128)(2,1)S(1)} async-done(((bf16[64,8,512]{2,1,0:T(8,128)(2,1)}), bf16[64,8,512]{2,1,0:T(8,128)(2,1)S(1)}, u32[]{:S(2)}, u32[]{:S(2)}) %all-to-all-start.4) | async-done | bytes 524320 | tf_op jit(solution)/shard_map/all_to_all | solution.py:311
  126.7 2.0 %blocks.3 = (bf16[512,512]{1,0:T(8,128)(2,1)S(1)}, bf16[128,512]{1,0:T(8,128)(2,1)S(1)}, f32[128,512]{1,0:T(8,128)S(1)}, f32[128,512]{1,0:T(8,128)S(1)}) custom-call(s32[2]{0:T(128)S(1)} %bitcast.49, s32[2]{0:T(128)S(1)} %bitcast.47, bf16[512,512]{1,0:T(8,128)(2,1)S(1)} %bitcast.37, f32[16,128]{1,0:T(8,128)S(1)} %get-tuple-element.37.rows_ref, ...), custom_call_target="tpu_custom_call" | custom-call | bytes 4194304 | tf_op jit(solution)/shard_map/blocks/pallas_call | solution.py:52
  128.8 23.4 %all_to_all.66 = bf16[64,8,512]{2,1,0:T(8,128)(2,1)S(1)} all-to-all(bf16[64,8,512]{2,1,0:T(8,128)(2,1)S(1)} %bitcast.42), channel_id=1, replica_groups=mesh['grp'=4,'wide'=64] {'wide'}, dimensions={0} | all-to-all | bytes 1048576 | tf_op jit(solution)/shard_map/all_to_all | solution.py:311
  152.2 1.0 broadcast_in_dim.25
  153.2 3.5 %all-to-all-start.6 = ((bf16[4,512,256]{2,1,0:T(8,128)(2,1)}), bf16[4,512,256]{2,1,0:T(8,128)(2,1)S(1)}, u32[]{:S(2)}, u32[]{:S(2)}) async-start(bf16[4,512,256]{2,1,0:T(8,128)(2,1)} %broadcast_in_dim.25), calls=%async_computation.6 | async-start | bytes 2097152 | tf_op jit(solution)/shard_map/all_to_all | solution.py:311
  156.7 0.0 copy-start.7
  156.8 1.0 ent_local.3.local_ref
  157.8 0.2 copy-done.7
  158.0 0.0 copy-start.5
  158.0 1.9 %ent_update.3 = (f32[500,512]{1,0:T(8,128)}, f32[1,512]{1,0:T(1,128)}) custom-call(s32[64,128]{1,0:T(8,128)S(1)} %bitcast.41, bf16[512,512]{1,0:T(8,128)(2,1)S(1)} %bitcast.33, f32[512,512]{1,0:T(8,128)S(1)} %ent_local.3.local_ref, f32[500,512]{1,0:T(8,128)S(1)} %copy-done.7, f32[1,512]{1,0:T(1,128)S(1)} %get-tuple-element.61.accum_ref), custom_call_target="tpu_custom_call" | custom-call | bytes 4194304 | tf_op jit(solution)/shard_map/ent_update/pallas_call | solution.py:52
  159.8 11.8 %all-to-all-done.6 = bf16[4,512,256]{2,1,0:T(8,128)(2,1)S(1)} async-done(((bf16[4,512,256]{2,1,0:T(8,128)(2,1)}), bf16[4,512,256]{2,1,0:T(8,128)(2,1)S(1)}, u32[]{:S(2)}, u32[]{:S(2)}) %all-to-all-start.6) | async-done | bytes 1048608 | tf_op jit(solution)/shard_map/all_to_all | solution.py:311
  171.6 0.0 copy-done.5
  171.6 2.7 %word_update.3 = (f32[500,512]{1,0:T(8,128)}, f32[1,512]{1,0:T(1,128)}) custom-call(bf16[2048,256]{1,0:T(8,128)(2,1)S(1)} %bitcast.26, f32[500,512]{1,0:T(8,128)S(1)} %copy-done.5, f32[1,512]{1,0:T(1,128)S(1)} %get-tuple-element.53.accum_ref), custom_call_target="tpu_custom_call" | custom-call | bytes 8388608 | tf_op jit(solution)/shard_map/word_update/pallas_call | solution.py:52
  (4 shorter events, 0.1 us)
Async XLA Ops:
  0.6 0.7 copy-start.13
  0.6 0.7 copy-start.14
  0.7 0.7 copy-start.12
  1.3 0.7 copy-start.15
  2.0 0.7 copy-start.16
  2.7 0.7 copy-start.17
  4.8 13.1 %copy-start.18 = (s32[2,2,512]{2,1,0:T(2,128)S(1)}, s32[2,2,512]{2,1,0:T(2,128)}, u32[]{:S(2)}) copy-start(s32[2,2,512]{2,1,0:T(2,128)} %param.25) | copy-start | bytes 24580
  4.8 22.3 %all-to-all-start = ((s32[64,1,128]{2,1,0:T(1,128)}), s32[64,1,128]{2,1,0:T(1,128)S(1)}, u32[]{:S(2)}, u32[]{:S(2)}) async-start(s32[64,1,128]{2,1,0:T(1,128)} %bitcast.5), calls=%async_computation | async-start | bytes 65536 | tf_op jit(solution)/shard_map/all_to_all | solution.py:311
  17.9 1.2 copy-start
  19.1 1.2 copy-start.2
  29.0 22.1 %all-to-all-start.1 = ((bf16[64,8,512]{2,1,0:T(8,128)(2,1)}), bf16[64,8,512]{2,1,0:T(8,128)(2,1)S(1)}, u32[]{:S(2)}, u32[]{:S(2)}) async-start(bf16[64,8,512]{2,1,0:T(8,128)(2,1)} %bitcast.9), calls=%async_computation.1 | async-start | bytes 1048576 | tf_op jit(solution)/shard_map/all_to_all | solution.py:311
  33.8 0.7 copy-start.8
  51.1 0.7 copy-start.9
  78.4 18.8 %all-to-all-start.3 = ((bf16[4,512,256]{2,1,0:T(8,128)(2,1)}), bf16[4,512,256]{2,1,0:T(8,128)(2,1)S(1)}, u32[]{:S(2)}, u32[]{:S(2)}) async-start(bf16[4,512,256]{2,1,0:T(8,128)(2,1)} %broadcast_in_dim.22), calls=%async_computation.3 | async-start | bytes 2097152 | tf_op jit(solution)/shard_map/all_to_all | solution.py:311
  82.5 1.2 copy-start.1
  82.5 1.2 copy-start.10
  83.8 13.4 %copy-start.3 = (f32[512,500]{0,1:T(8,128)S(1)}, f32[512,500]{0,1:T(8,128)}, u32[]{:S(2)}) copy-start(f32[512,500]{0,1:T(8,128)} %param.13) | copy-start | bytes 3072004
  84.8 1.0 copy-start.6
  97.1 0.7 copy-start.11
  101.3 1.0 copy-start.4
  102.3 24.4 %all-to-all-start.4 = ((bf16[64,8,512]{2,1,0:T(8,128)(2,1)}), bf16[64,8,512]{2,1,0:T(8,128)(2,1)S(1)}, u32[]{:S(2)}, u32[]{:S(2)}) async-start(bf16[64,8,512]{2,1,0:T(8,128)(2,1)} %bitcast.16), calls=%async_computation.4 | async-start | bytes 1048576 | tf_op jit(solution)/shard_map/all_to_all | solution.py:311
  153.2 18.4 %all-to-all-start.6 = ((bf16[4,512,256]{2,1,0:T(8,128)(2,1)}), bf16[4,512,256]{2,1,0:T(8,128)(2,1)S(1)}, u32[]{:S(2)}, u32[]{:S(2)}) async-start(bf16[4,512,256]{2,1,0:T(8,128)(2,1)} %broadcast_in_dim.25), calls=%async_computation.6 | async-start | bytes 2097152 | tf_op jit(solution)/shard_map/all_to_all | solution.py:311
  156.7 1.2 copy-start.7
  158.0 13.6 %copy-start.5 = (f32[500,512]{1,0:T(8,128)S(1)}, f32[500,512]{1,0:T(8,128)}, u32[]{:S(2)}) copy-start(f32[500,512]{1,0:T(8,128)} %copy-done.4) | copy-start | bytes 3072004
where the time goes:
time: 175 us; the launch traced here: 174 us
  waiting for transfers between devices  60.3 us (34%)
  blocking collectives  46.9 us (27%)
  starting transfers between devices  32.6 us (19%)
  Pallas kernels  22.1 us (13%)
  local copies, waits for them, and re-layouts  11.6 us (7%)
    all_to_all x5, waiting for transfers between devices, exchange(): return lax.all_to_all(x, axis, split_axis=0, concat_axis=0, tiled=True)  60.3 us
    all_to_all x2, blocking collectives, exchange(): return lax.all_to_all(x, axis, split_axis=0, concat_axis=0, tiled=True)  46.9 us
    all_to_all x5, starting transfers between devices, exchange(): return lax.all_to_all(x, axis, split_axis=0, concat_axis=0, tiled=True)  32.6 us
    pallas_call x13, Pallas kernels, kernel_call(): pl.pallas_call(body, out_shape=out_shape, in_specs=in_specs, out_specs=ou...  22.1 us
    unnamed x38, local copies, waits for them, and re-layouts  9.46 us
  transfers between devices with their start and end apart: 5, of which 5 were waited for; matrix products, arithmetic and copies ran while one was open for 0% of the time, Pallas kernels for 5%

commit v1 on v0

v1 whole, which is shorter than its diff:
```python
import functools

import jax
import jax.numpy as jnp
from jax import lax
from jax.experimental import pallas as pl
from jax.experimental.pallas import tpu as pltpu
from jax.sharding import PartitionSpec as P

BLOCK = 128
STEPS = 2
LEARN = 0.1
CAP = 4
HALF = 256
CUT = 248
PAD = 2 * HALF
ID_HI = 252
ID_LO = 253
F32 = jnp.float32
BF16 = jnp.bfloat16

PLACE_W, PLACE_L, RANK_W, RANK_L, WORD_ROW, LINK_ROW, ANCHOR_ENT, LINK_SRC, MASK_W, MASK_L = range(10)
STRIDE = 16


def iota(shape, dim):
    return lax.broadcasted_iota(jnp.int32, shape, dim).astype(F32)


def nn(a, b):
    return lax.dot_general(a, b, (((1,), (0,)), ((), ())), preferred_element_type=F32)


def nt(a, b):
    return lax.dot_general(a, b, (((1,), (1,)), ((), ())), preferred_element_type=F32)


def hot(condition):
    return jnp.where(condition, 1.0, 0.0).astype(BF16)


def split(x):
    high = x.astype(BF16)
    return high, (x - high.astype(F32)).astype(BF16)


def kernel_call(body, out_shape, name, operands, scratch=(), hbm=(), hbm_out=(), moved=0, pin=False):
    if pin:
        operands = [pltpu.with_memory_space_constraint(x, pltpu.HBM) for x in operands]

    def space(far):
        return pl.BlockSpec(memory_space=pltpu.HBM if far else pltpu.VMEM)

    return pl.pallas_call(
        body,
        out_shape=out_shape,
        in_specs=[space(i in hbm) for i in range(len(operands))],
        out_specs=tuple(space(i in hbm_out) for i in range(len(out_shape))),
        scratch_shapes=list(scratch),
        name=name,
        compiler_params=pltpu.CompilerParams(vmem_limit_bytes=32 * 2**20),
        cost_estimate=pl.CostEstimate(flops=0, bytes_accessed=moved, transcendentals=0),
    )(*operands)


def fetch(sources, targets, sems):
    copies = [
        pltpu.make_async_copy(source, target, sems.at[i])
        for i, (source, target) in enumerate(zip(sources, targets))
    ]
    for copy in copies:
        copy.start()
    for copy in copies:
        copy.wait()


def prepare_body(*refs):
    sources, (asks_ref, rows_ref, cols_ref), (*held, table, sems) = refs[:8], refs[8:11], refs[11:]
    fetch(sources, held, sems)
    aws, lds, awr, ldr, aer, lsr, anchor_count, link_count = held
    peers = asks_ref.shape[0]
    table[...] = jnp.zeros_like(table)
    earlier = hot(iota((BLOCK, BLOCK), 0) < iota((BLOCK, BLOCK), 1))
    peer = iota((peers, BLOCK), 0)
    spot = iota((1, BLOCK), 1)

    def note(step, which, value):
        table[STRIDE * step + which : STRIDE * step + which + 1, :] = value

    kinds = [(step, kind) for step in range(STEPS) for kind in range(2)]
    shards = [(aws, lds)[kind][step : step + 1, :].astype(F32) for step, kind in kinds]
    owners = [peer == shard for shard in shards]
    owned = [hot(owner) for owner in owners]
    before = nn(jnp.concatenate(owned, axis=0), earlier)
    for i, (step, kind) in enumerate(kinds):
        counted = before[i * peers : (i + 1) * peers, :]
        rank = jnp.sum(jnp.where(owners[i], counted, 0.0), axis=0, keepdims=True)
        note(step, PLACE_W + kind, shards[i] * (2 * CAP) + rank)
        note(step, RANK_W + kind, rank)
        note(step, WORD_ROW + kind, (awr, ldr)[kind][step : step + 1, :].astype(F32))
        limit = (anchor_count, link_count)[kind][0:1, step : step + 1].astype(F32)
        note(step, MASK_W + kind, jnp.where(spot < limit, 1.0, 0.0))
    for step in range(STEPS):
        note(step, ANCHOR_ENT, aer[step : step + 1, :].astype(F32))
        note(step, LINK_SRC, lsr[step : step + 1, :].astype(F32))
    rows_ref[...] = table[0 : STEPS * STRIDE, :]
    cols = jnp.transpose(table[...])
    cols_ref[...] = cols
    lane = iota((BLOCK, BLOCK), 1)
    values = []
    for i, (step, kind) in enumerate(kinds):
        base = STRIDE * step + kind
        rank = cols[:, base + RANK_W : base + RANK_W + 1]
        row = cols[:, base + WORD_ROW : base + WORD_ROW + 1]
        high = jnp.floor(row * (1.0 / 16.0))
        place = i * CAP + rank
        value = jnp.where(
            lane == place, high, jnp.where(lane == place + 64.0, row - 16.0 * high, 0.0)
        )
        values.append(value.astype(BF16))
    asks = nn(jnp.concatenate(owned, axis=1), jnp.concatenate(values, axis=0))
    asks_ref[...] = asks.astype(jnp.int32)


def to_half(ref, out_ref, scratch):
    scratch[CUT:HALF, :] = jnp.zeros((HALF - CUT, scratch.shape[1]), F32)
    scratch[PAD - 8 : PAD, :] = jnp.zeros((8, scratch.shape[1]), F32)
    scratch[0:CUT, :] = ref[0:CUT, :]
    scratch[HALF : HALF + ref.shape[0] - CUT, :] = ref[CUT:, :]
    out_ref[...] = scratch[...].astype(BF16)


def halves_body(
    ent_hbm,
    word_hbm,
    neg_hbm,
    ent_sum_hbm,
    word_sum_hbm,
    ent_out,
    word_out,
    counts_out,
    ent_sum_out,
    word_sum_out,
    ent,
    word,
    neg,
    scratch,
    sems,
):
    fetch(
        (neg_hbm, ent_hbm, word_hbm, ent_sum_hbm, word_sum_hbm),
        (neg, ent, word, ent_sum_out, word_sum_out),
        sems,
    )
    to_half(ent, ent_out, scratch)
    to_half(word, word_out, scratch)
    entity = iota((ent.shape[1], neg.shape[-1]), 0)
    ones = jnp.ones((8, neg.shape[-1]), BF16)
    for i in range(2 * STEPS):
        named = hot(entity == neg[i // 2, i % 2 : i % 2 + 1, :].astype(F32))
        counts_out[8 * i : 8 * i + 8, :] = nt(ones, named)


def id_column(asks_ref, which):
    peers = asks_ref.shape[0]
    rows = peers * 2 * CAP
    source = hot(
        lax.broadcasted_iota(jnp.int32, (rows, peers), 0) // (2 * CAP)
        == lax.broadcasted_iota(jnp.int32, (rows, peers), 1)
    )
    spread = nn(source, asks_ref[...].astype(BF16))
    lane = lax.broadcasted_iota(jnp.int32, (rows, BLOCK), 1)
    place = which * CAP + lax.broadcasted_iota(jnp.int32, (rows, BLOCK), 0) % CAP
    weight = jnp.where(lane == place, 16.0, jnp.where(lane == place + 64, 1.0, 0.0))
    return jnp.sum(spread * weight, axis=1, keepdims=True)


def first_half(rows):
    return lax.broadcasted_iota(jnp.int32, (rows, HALF), 0) % (2 * CAP) < CAP


def named_rows(ids, count):
    return hot(iota((ids.shape[0], count), 1) == ids)


def lookup(named, half_ref):
    both = nt(named, half_ref[...])
    return jnp.where(first_half(named.shape[0]), both[:, 0:HALF], both[:, HALF:]).astype(BF16)


def column(cols_ref, step, which):
    return cols_ref[:, STRIDE * step + which : STRIDE * step + which + 1]


def row_of(rows_ref, step, which):
    return rows_ref[STRIDE * step + which : STRIDE * step + which + 1, :]


def sigmoid(x):
    return jax.nn.sigmoid(x)


def product(coef, half_ref):
    high, low = split(coef)
    both = nt(jnp.concatenate([high, low], axis=0), half_ref[...])
    return both[0 : coef.shape[0], :] + both[coef.shape[0] :, :]


def sources(step, cols_ref, ent_half):
    named = hot(iota((BLOCK, ent_half.shape[1]), 1) == column(cols_ref, step, LINK_SRC))
    return named, nt(named, ent_half[...]).astype(BF16)


def link_send(step, asks_ref, rows_ref, cols_ref, ent_half, out_ref, start):
    ids = id_column(asks_ref, 2 * step + 1)
    out_ref[:, start : start + HALF] = lookup(named_rows(ids, ent_half.shape[1]), ent_half)
    place = jnp.where(
        row_of(rows_ref, step, MASK_L) > 0.0, row_of(rows_ref, step, PLACE_L), -float(2 * CAP)
    )
    _, src = sources(step, cols_ref, ent_half)
    out_ref[:, start + HALF : start + PAD] = put(
        place, src[:, 0:HALF], src[:, HALF:PAD], out_ref.shape[0]
    ).astype(BF16)


def respond_body(asks_ref, rows_ref, cols_ref, word_half, ent_half, out_ref):
    named = named_rows(id_column(asks_ref, 0), word_half.shape[1])
    out_ref[:, 0:HALF] = lookup(named, word_half)
    link_send(0, asks_ref, rows_ref, cols_ref, ent_half, out_ref, HALF)


def take(recv, place):
    rows = recv.shape[0]
    lane = iota((2 * BLOCK, rows), 1)
    named = hot(lane == jnp.concatenate([place, place + CAP], axis=0))
    both = nn(named, recv)
    return jnp.concatenate([both[0:BLOCK, :], both[BLOCK:, :]], axis=1)


def put(place, low, high, rows):
    row = iota((rows, 2 * BLOCK), 0)
    named = hot(row == jnp.concatenate([place, place + CAP], axis=1))
    return nn(named, jnp.concatenate([low, high], axis=0))


def anchor_coefficients(step, words, cols_ref, counts_ref, ent_half):
    mask = column(cols_ref, step, MASK_W)
    score = nn(words, ent_half[...])
    target = iota(score.shape, 1) == column(cols_ref, step, ANCHOR_ENT)
    pos = jnp.sum(jnp.where(target, score, 0.0), axis=1, keepdims=True)
    pull = mask * (sigmoid(pos) - 1.0)
    push = (mask * sigmoid(score)).astype(BF16).astype(F32)
    return push * counts_ref[16 * step : 16 * step + 1, :] + jnp.where(target, pull, 0.0)


def anchor_body(step, recv_ref, rows_ref, cols_ref, counts_ref, ent_half, send_ref):
    words = take(recv_ref[:, 0:HALF], column(cols_ref, step, PLACE_W)).astype(BF16)
    centre = product(anchor_coefficients(step, words, cols_ref, counts_ref, ent_half), ent_half)
    word_row = column(cols_ref, step, WORD_ROW)
    id_high = jnp.floor(word_row * (1.0 / 16.0))
    lane = lax.broadcasted_iota(jnp.int32, (BLOCK, PAD), 1) % HALF
    centre = jnp.where(
        lane == ID_HI, id_high, jnp.where(lane == ID_LO, word_row - 16.0 * id_high, centre)
    ).astype(BF16)
    place = row_of(rows_ref, step, PLACE_W)
    send_ref[...] = put(place, centre[:, 0:HALF], centre[:, HALF:PAD], send_ref.shape[0]).astype(BF16)


def adagrad(table_ref, accum, low, high):
    width = table_ref.shape[0]
    low = low[0:CUT, :]
    high = high[0 : width - CUT, :]
    square = jnp.sum(low * low, axis=0, keepdims=True) + jnp.sum(high * high, axis=0, keepdims=True)
    accum = accum + square * (1.0 / width)
    rate = LEARN * lax.rsqrt(accum)
    table_ref[0:CUT, :] = table_ref[0:CUT, :] - low * rate
    table_ref[CUT:, :] = table_ref[CUT:, :] - high * rate
    return accum


def ent_update_body(
    step,
    last,
    link_at,
    asks_ref,
    rows_ref,
    cols_ref,
    counts_ref,
    recv_ref,
    link_recv,
    ent_half,
    table_hbm,
    accum_ref,
    table_out,
    accum_out,
    *rest,
):
    if last:
        table, sems = rest
    else:
        half_out, links_out, table, scratch, sems = rest
    rows = recv_ref.shape[0]
    table_in = pltpu.make_async_copy(table_hbm, table, sems.at[0])
    table_in.start()
    words = take(recv_ref[:, 0:HALF], column(cols_ref, step, PLACE_W)).astype(BF16)
    coef = anchor_coefficients(step, words, cols_ref, counts_ref, ent_half)
    source, src = sources(step, cols_ref, ent_half)
    mask = column(cols_ref, step, MASK_L)
    push = (mask * sigmoid(nn(src, ent_half[...]))).astype(BF16).astype(F32)
    link_coef = push * counts_ref[16 * step + 8 : 16 * step + 9, :]
    targets = take(link_recv[:, link_at : link_at + HALF], column(cols_ref, step, PLACE_L))
    src_float = src.astype(F32)
    pos = jnp.sum(src_float * targets, axis=1, keepdims=True)
    pull = mask * (sigmoid(pos) - 1.0)
    link_grad = pull * targets + product(link_coef, ent_half)
    centres = jnp.concatenate([words.astype(F32), src_float], axis=0)
    centres = jnp.transpose(centres).astype(BF16)
    high, low = split(jnp.concatenate([coef, link_coef], axis=0))
    total = nn(centres, high) + nn(centres, low)
    high, low = split(jnp.transpose(link_grad))
    total = total + nn(high, source) + nn(low, source)
    named = named_rows(id_column(asks_ref, 2 * step + 1), ent_half.shape[1])
    pushed = jnp.transpose(link_recv[:, link_at + HALF :].astype(F32))
    lower = lax.broadcasted_iota(jnp.int32, (1, rows), 1) % (2 * CAP) < CAP
    held = jnp.where(lower, nt(ent_half[0:HALF, :], named), nt(ent_half[HALF:PAD, :], named))
    part = jnp.sum(pushed * held, axis=0, keepdims=True)
    other = jnp.where(lower, jnp.roll(part, -CAP, axis=1), jnp.roll(part, CAP, axis=1))
    grads = (sigmoid(part + other) - 1.0) * pushed
    low = nn(jnp.where(lower, grads, 0.0).astype(BF16), named) + total[0:HALF, :]
    high = nn(jnp.where(lower, 0.0, grads).astype(BF16), named) + total[HALF:PAD, :]
    table_in.wait()
    accum_out[...] = adagrad(table, accum_ref[...], low, high)
    table_done = pltpu.make_async_copy(table, table_out, sems.at[0])
    table_done.start()
    if not last:
        to_half(table, half_out, scratch)
        link_send(step + 1, asks_ref, rows_ref, cols_ref, half_out, links_out, 0)
    table_done.wait()


def compact_body(recv_ref, out_ref):
    rows = recv_ref.shape[0]
    places = out_ref.shape[1]
    grads = jnp.transpose(recv_ref[...].astype(F32)).astype(BF16)
    row = lax.broadcasted_iota(jnp.int32, (rows, places), 0)
    place = lax.broadcasted_iota(jnp.int32, (rows, places), 1)
    place = place // CAP * (2 * CAP) + place % CAP
    low = nn(grads, hot(row == place))
    high = nn(grads, hot(row == place + CAP))
    out_ref[...] = jnp.concatenate([low[0:CUT, :], high], axis=0).astype(BF16)


def word_gradient(recv_ref, count):
    groups, depth, places = recv_ref.shape
    columns = jnp.concatenate([recv_ref[group] for group in range(groups)], axis=1)
    ids = columns[depth - 8 :, :].astype(F32)
    ids = ids[4:5, :] * 16.0 + ids[5:6, :]
    return nt(columns, hot(iota((count, groups * places), 0) == ids))


def word_update_body(
    step,
    asks_ref,
    recv_ref,
    table_hbm,
    accum_ref,
    table_out,
    accum_out,
    send_ref,
    table,
    half,
    scratch,
    sem,
):
    table_in = pltpu.make_async_copy(table_hbm, table, sem)
    table_in.start()
    named = named_rows(id_column(asks_ref, 2 * step + 2), table.shape[1])
    total = word_gradient(recv_ref, table.shape[1])
    table_in.wait()
    accum_out[...] = adagrad(table, accum_ref[...], total[0:CUT, :], total[CUT:, :])
    table_done = pltpu.make_async_copy(table, table_out, sem)
    table_done.start()
    to_half(table, half, scratch)
    send_ref[...] = lookup(named, half)
    table_done.wait()


def word_final_body(recv_ref, table_ref, accum_ref, table_out, accum_out):
    width, words = table_ref.shape
    grad = word_gradient(recv_ref, words)[0:width, :]
    accum = accum_ref[...] + jnp.sum(grad * grad, axis=0, keepdims=True) * (1.0 / width)
    accum_out[...] = accum
    table_out[...] = table_ref[...] - grad * (LEARN * lax.rsqrt(accum))


def shape(*dims, dtype=F32):
    return jax.ShapeDtypeStruct(dims, dtype)


def exchange(x):
    return lax.all_to_all(x, "wide", split_axis=0, concat_axis=0, tiled=True)


def on_device(
    word_table,
    word_accum,
    ent_table,
    ent_accum,
    anchor_word_shard,
    anchor_word_row,
    anchor_ent_row,
    anchor_count,
    link_src_row,
    link_dst_shard,
    link_dst_row,
    link_count,
    neg_rows,
):
    peers = lax.axis_size("wide")
    message = peers * 2 * CAP
    word, ent = word_table.T, ent_table.T
    word_sum, ent_sum = word_accum[None, :], ent_accum[None, :]
    width, words = word.shape
    entities = ent.shape[1]
    indices = (
        anchor_word_shard[:, :, 0],
        link_dst_shard[:, :, 0],
        anchor_word_row,
        link_dst_row,
        anchor_ent_row,
        link_src_row,
        anchor_count.T,
        link_count.T,
    )
    asks, rows, cols = kernel_call(
        prepare_body,
        (shape(peers, BLOCK, dtype=jnp.int32), shape(STEPS * STRIDE, BLOCK), shape(BLOCK, BLOCK)),
        "prepare",
        indices,
        scratch=[pltpu.VMEM(x.shape, jnp.int32) for x in indices]
        + [pltpu.VMEM((BLOCK, BLOCK), F32), pltpu.SemaphoreType.DMA((len(indices),))],
        hbm=range(len(indices)),
        moved=2**18,
        pin=True,
    )
    asked = exchange(asks[:, None, :])[:, 0, :]
    half_shape = shape(PAD, entities, dtype=BF16)
    ent_half, word_half, counts, ent_sum, word_sum = kernel_call(
        halves_body,
        (
            half_shape,
            shape(PAD, words, dtype=BF16),
            shape(8 * 2 * STEPS, entities),
            shape(1, entities),
            shape(1, words),
        ),
        "halves",
        (ent, word, neg_rows, ent_sum, word_sum),
        scratch=(
            pltpu.VMEM(ent.shape, F32),
            pltpu.VMEM(word.shape, F32),
            pltpu.VMEM(neg_rows.shape, jnp.int32),
            pltpu.VMEM((PAD, entities), F32),
            pltpu.SemaphoreType.DMA((5,)),
        ),
        hbm=range(5),
        moved=2**22,
    )
    send_shape = shape(message, 3 * HALF, dtype=BF16)
    links_shape = shape(message, PAD, dtype=BF16)
    (send,) = kernel_call(
        respond_body,
        (send_shape,),
        "respond",
        (asked, rows, cols, word_half, ent_half),
        moved=2**22,
    )
    for step in range(STEPS):
        last = step == STEPS - 1
        recv = exchange(send)
        if step == 0:
            link_recv, link_at = recv, HALF
        (grads,) = kernel_call(
            functools.partial(anchor_body, step),
            (shape(message, HALF, dtype=BF16),),
            "anchor",
            (recv, rows, cols, counts, ent_half),
            moved=2**22,
        )
        received = exchange(grads)
        held = (pltpu.VMEM((width, entities), F32),)
        out = kernel_call(
            functools.partial(ent_update_body, step, last, link_at),
            (shape(width, entities), shape(1, entities)) + (() if last else (half_shape, links_shape)),
            "ent_update",
            (asked, rows, cols, counts, recv, link_recv, ent_half, ent, ent_sum),
            scratch=held
            + (
                ()
                if last
                else (pltpu.VMEM((PAD, entities), F32),)
            )
            + (pltpu.SemaphoreType.DMA((1,)),),
            hbm=(7,),
            hbm_out=(0,),
            moved=2**23,
        )
        ent, ent_sum = out[0], out[1]
        if not last:
            ent_half = out[2]
            received, links = lax.optimization_barrier((received, out[3]))
            link_recv, link_at = exchange(links), 0
        (mine,) = kernel_call(
            compact_body,
            (shape(CUT + HALF, peers * CAP, dtype=BF16),),
            "compact",
            (received,),
            moved=2**20,
        )
        every = lax.all_gather(mine, "grp", axis=0, tiled=False)
        if last:
            word, word_sum = kernel_call(
                word_final_body,
                (shape(width, words), shape(1, words)),
                "word_final",
                (every, word, word_sum),
                moved=2**23,
            )
        else:
            word, word_sum, send = kernel_call(
                functools.partial(word_update_body, step),
                (shape(width, words), shape(1, words), shape(message, HALF, dtype=BF16)),
                "word_update",
                (asked, every, word, word_sum),
                scratch=(
                    pltpu.VMEM((width, words), F32),
                    pltpu.VMEM((PAD, words), BF16),
                    pltpu.VMEM((PAD, words), F32),
                    pltpu.SemaphoreType.DMA,
                ),
                hbm=(2,),
                hbm_out=(0,),
                moved=2**23,
            )
            send, link_recv = lax.optimization_barrier((send, link_recv))
    return (word.T, word_sum[0], ent.T, ent_sum[0])


def solution(mesh):
    in_specs = (
        P("wide", None),
        P("wide"),
        P(("grp", "wide"), None),
        P(("grp", "wide")),
        P(None, ("grp", "wide"), None),
        P(None, ("grp", "wide")),
        P(None, ("grp", "wide")),
        P(None, ("grp", "wide")),
        P(None, ("grp", "wide")),
        P(None, ("grp", "wide"), None),
        P(None, ("grp", "wide")),
        P(None, ("grp", "wide")),
        P(None, ("grp", "wide"), None),
    )
    out_specs = (P("wide", None), P("wide"), P(("grp", "wide"), None), P(("grp", "wide")))
    return jax.shard_map(
        on_device, mesh=mesh, in_specs=in_specs, out_specs=out_specs, check_vma=False
    )
```

time: 175 us -> 159 us (0.909)
  waiting for transfers between devices: 60.3 us -> 17.3 us
  blocking collectives: 46.9 us -> 78.6 us
  local copies, waits for them, and re-layouts: 11.6 us -> 6.09 us
    all_to_all x5 -> x4, waiting for transfers between devices: 60.3 us -> 17.3 us  [exchange(): return lax.all_to_all(x, 'wide', split_axis=0, concat_axis=0, tiled=True)]
    all_gather x0 -> x2, blocking collectives: none -> 27.5 us  [on_device(): every = lax.all_gather(mine, 'grp', axis=0, tiled=False)]
    all_to_all x2, blocking collectives: 46.9 us -> 51 us  [exchange(): return lax.all_to_all(x, 'wide', split_axis=0, concat_axis=0, tiled=True)]
    unnamed x38 -> x20, local copies, waits for them, and re-layouts: 9.46 us -> 6.09 us
    broadcast_in_dim x2 -> x0, local copies, waits for them, and re-layouts: 2.07 us -> none  [on_device(): mine = jnp.broadcast_to(received[None, :, 0:HALF], (groups, message, HALF))]
    all_to_all x5 -> x4, starting transfers between devices: 32.6 us -> 31.2 us  [exchange(): return lax.all_to_all(x, 'wide', split_axis=0, concat_axis=0, tiled=True)]
    pallas_call x13 -> x11, Pallas kernels: 22.1 us -> 23.3 us  [kernel_call(): pl.pallas_call(body, out_shape=out_shape, in_specs=[space(i in hbm) for i...]
  transfers between devices with their start and end apart: 5 -> 4, of which waited for: 5 -> 4; matrix products, arithmetic and copies ran while one was open for 0% -> 0% of each run, Pallas kernels for 5% -> 9%
where the time goes in v1:
time: 159 us; the launch traced here: 157 us
  blocking collectives  78.6 us (49%)
  starting transfers between devices  31.2 us (20%)
  Pallas kernels  23.3 us (15%)
  waiting for transfers between devices  17.3 us (11%)
  local copies, waits for them, and re-layouts  6.09 us (4%)
    all_to_all x2, blocking collectives, exchange(): return lax.all_to_all(x, 'wide', split_axis=0, concat_axis=0, tiled=True)  51 us
    all_to_all x4, starting transfers between devices, exchange(): return lax.all_to_all(x, 'wide', split_axis=0, concat_axis=0, tiled=True)  31.2 us
    all_gather x2, blocking collectives, on_device(): every = lax.all_gather(mine, 'grp', axis=0, tiled=False)  27.5 us
    pallas_call x11, Pallas kernels, kernel_call(): pl.pallas_call(body, out_shape=out_shape, in_specs=[space(i in hbm) for i...  23.3 us
    all_to_all x4, waiting for transfers between devices, exchange(): return lax.all_to_all(x, 'wide', split_axis=0, concat_axis=0, tiled=True)  17.3 us
    unnamed x20, local copies, waits for them, and re-layouts  6.09 us
  transfers between devices with their start and end apart: 4, of which 4 were waited for; matrix products, arithmetic and copies ran while one was open for 0% of the time, Pallas kernels for 9%

profile of v1, /device:TPU:1, one launch (start us, length us, event | category | flops | bytes accessed | tf_op | source)
XLA Modules:
  0.0 157.3 jit_solution(11194022472847879770)
XLA Ops:
  0.6 2.2 %prepare.1 = (s32[64,128]{1,0:T(8,128)}, f32[32,128]{1,0:T(8,128)S(1)}, f32[128,128]{1,0:T(8,128)S(1)}) custom-call(s32[2,128]{1,0:T(2,128)} %bitcast.51, s32[2,128]{1,0:T(2,128)} %bitcast.52, s32[2,128]{1,0:T(2,128)} %refs_2_.1, s32[2,128]{1,0:T(2,128)} %refs_3_.1, s32[2,128]{1,0:T(2,128)} %refs_4_.1, s32[2,128]{1,0:T(2,128)} %refs_5_.1, s32[1,2]{1,0:T(1,128)} %bitcast.53, ...), custom_call_target="tpu_custom_call" | custom-call | bytes 262144 | tf_op jit(solution)/shard_map/prepare/pallas_call | solution.py:54
  2.9 0.0 copy-start.7
  2.9 13.0 %all-to-all-start = ((s32[64,1,128]{2,1,0:T(1,128)}), s32[64,1,128]{2,1,0:T(1,128)S(1)}, u32[]{:S(2)}, u32[]{:S(2)}) async-start(s32[64,1,128]{2,1,0:T(1,128)} %bitcast.5), calls=%async_computation | async-start | bytes 65536 | tf_op jit(solution)/shard_map/all_to_all | solution.py:401
  15.9 0.0 copy-start.9
  15.9 0.0 copy-start.8
  15.9 0.0 copy-done.7
  15.9 0.7 copy-done.9
  16.6 0.0 copy-done.8
  16.6 0.0 copy-start
  16.6 1.2 copy-done
  17.8 0.0 copy-start.2
  17.8 1.2 copy-done.2
  19.0 1.6 halves.1
  20.6 4.5 %all-to-all-done = s32[64,1,128]{2,1,0:T(1,128)S(1)} async-done(((s32[64,1,128]{2,1,0:T(1,128)}), s32[64,1,128]{2,1,0:T(1,128)S(1)}, u32[]{:S(2)}, u32[]{:S(2)}) %all-to-all-start) | async-done | bytes 32800 | tf_op jit(solution)/shard_map/all_to_all | solution.py:401
  25.1 1.5 respond.1
  26.6 28.6 %all_to_all.62 = bf16[64,8,768]{2,1,0:T(8,128)(2,1)S(1)} all-to-all(bf16[64,8,768]{2,1,0:T(8,128)(2,1)S(1)} %bitcast.37), channel_id=1, replica_groups=mesh['grp'=4,'wide'=64] {'wide'}, dimensions={0} | all-to-all | bytes 1572864 | tf_op jit(solution)/shard_map/all_to_all | solution.py:401
  55.2 0.0 copy-start.1
  55.2 1.9 %anchor.2 = bf16[512,256]{1,0:T(8,128)(2,1)} custom-call(bf16[512,768]{1,0:T(8,128)(2,1)S(1)} %bitcast.28, f32[32,128]{1,0:T(8,128)S(1)} %get-tuple-element.28.rows_ref, f32[128,128]{1,0:T(8,128)S(1)} %get-tuple-element.29.cols_ref, f32[32,512]{1,0:T(8,128)S(1)} %get-tuple-element.32.counts_ref, bf16[512,512]{1,0:T(8,128)(2,1)S(1)} %get-tuple-element.31.ent_half), custom_call_target="tpu_custom_call" | custom-call | bytes 4194304 | tf_op jit(solution)/shard_map/anchor/pallas_call | solution.py:54
  57.1 6.2 %all-to-all-start.2 = ((bf16[64,8,256]{2,1,0:T(8,128)(2,1)}), bf16[64,8,256]{2,1,0:T(8,128)(2,1)S(1)}, u32[]{:S(2)}, u32[]{:S(2)}) async-start(bf16[64,8,256]{2,1,0:T(8,128)(2,1)} %bitcast.13), calls=%async_computation.2 | async-start | bytes 524288 | tf_op jit(solution)/shard_map/all_to_all | solution.py:401
  63.3 0.0 copy-done.1
  63.3 4.6 %ent_update.2 = (f32[500,512]{1,0:T(8,128)S(1)}, f32[1,512]{1,0:T(1,128)S(1)}, bf16[512,512]{1,0:T(8,128)(2,1)S(1)}, bf16[512,512]{1,0:T(8,128)(2,1)S(1)}) custom-call(s32[64,128]{1,0:T(8,128)S(1)} %bitcast.44, f32[32,128]{1,0:T(8,128)S(1)} %get-tuple-element.28.rows_ref, f32[128,128]{1,0:T(8,128)S(1)} %get-tuple-element.29.cols_ref, ...), custom_call_target="tpu_custom_call" | custom-call | bytes 8388608 | tf_op jit(solution)/shard_map/ent_update/pallas_call | solution.py:54
  68.0 0.0 copy-start.4
  68.0 1.0 copy-done.4
  68.9 0.0 copy-start.6
  68.9 0.8 copy-done.6
  69.7 5.6 %all-to-all-done.2 = bf16[64,8,256]{2,1,0:T(8,128)(2,1)S(1)} async-done(((bf16[64,8,256]{2,1,0:T(8,128)(2,1)}), bf16[64,8,256]{2,1,0:T(8,128)(2,1)S(1)}, u32[]{:S(2)}, u32[]{:S(2)}) %all-to-all-start.2) | async-done | bytes 262176 | tf_op jit(solution)/shard_map/all_to_all | solution.py:401
  75.3 6.0 %all-to-all-start.3 = ((bf16[64,8,512]{2,1,0:T(8,128)(2,1)}), bf16[64,8,512]{2,1,0:T(8,128)(2,1)S(1)}, u32[]{:S(2)}, u32[]{:S(2)}) async-start(bf16[64,8,512]{2,1,0:T(8,128)(2,1)} %bitcast.47), calls=%async_computation.3 | async-start | bytes 1048576 | tf_op jit(solution)/shard_map/all_to_all | solution.py:401
  81.4 0.0 copy-start.3
  81.4 0.4 compact.2
  81.8 13.6 %all-gather = bf16[2016,256]{1,0:T(8,128)(2,1)S(1)} all-gather(bf16[504,256]{1,0:T(8,128)(2,1)S(1)} %compact.2), channel_id=2, replica_groups=mesh['grp'=4,'wide'=64] {'grp'}, dimensions={0}, use_global_device_ids=true | all-gather | bytes 1290240 | tf_op jit(solution)/shard_map/all_gather | solution.py:520
  95.4 0.0 copy-done.3
  95.4 2.2 %word_update.1 = (f32[500,512]{1,0:T(8,128)S(1)}, f32[1,512]{1,0:T(1,128)S(1)}, bf16[512,256]{1,0:T(8,128)(2,1)S(1)}) custom-call(s32[64,128]{1,0:T(8,128)S(1)} %bitcast.45, bf16[4,504,256]{2,1,0:T(8,128)(2,1)S(1)} %bitcast.31, f32[500,512]{1,0:T(8,128)S(1)} %bitcast.36, f32[1,512]{1,0:T(1,128)S(1)} %get-tuple-element.36.accum_ref), custom_call_target="tpu_custom_call" | custom-call | bytes 8388608 | tf_op jit(solution)/shard_map/word_update/pallas_call | solution.py:54
  97.6 1.1 all-to-all-done.3
  98.7 22.4 %all_to_all.63 = bf16[64,8,256]{2,1,0:T(8,128)(2,1)S(1)} all-to-all(bf16[64,8,256]{2,1,0:T(8,128)(2,1)S(1)} %bitcast.48), channel_id=1, replica_groups=mesh['grp'=4,'wide'=64] {'wide'}, dimensions={0} | all-to-all | bytes 524288 | tf_op jit(solution)/shard_map/all_to_all | solution.py:401
  121.1 1.9 %anchor.3 = bf16[512,256]{1,0:T(8,128)(2,1)} custom-call(bf16[512,256]{1,0:T(8,128)(2,1)S(1)} %bitcast.38, f32[32,128]{1,0:T(8,128)S(1)} %get-tuple-element.28.rows_ref, f32[128,128]{1,0:T(8,128)S(1)} %get-tuple-element.29.cols_ref, f32[32,512]{1,0:T(8,128)S(1)} %get-tuple-element.32.counts_ref, bf16[512,512]{1,0:T(8,128)(2,1)S(1)} %get-tuple-element.40.ent_half), custom_call_target="tpu_custom_call" | custom-call | bytes 4194304 | tf_op jit(solution)/shard_map/anchor/pallas_call | solution.py:54
  123.0 6.0 %all-to-all-start.5 = ((bf16[64,8,256]{2,1,0:T(8,128)(2,1)}), bf16[64,8,256]{2,1,0:T(8,128)(2,1)S(1)}, u32[]{:S(2)}, u32[]{:S(2)}) async-start(bf16[64,8,256]{2,1,0:T(8,128)(2,1)} %bitcast.20), calls=%async_computation.5 | async-start | bytes 524288 | tf_op jit(solution)/shard_map/all_to_all | solution.py:401
  129.1 0.0 copy-start.5
  129.1 1.2 copy-done.5
  130.3 4.8 %ent_update.3 = (f32[500,512]{1,0:T(8,128)}, f32[1,512]{1,0:T(1,128)}) custom-call(s32[64,128]{1,0:T(8,128)S(1)} %bitcast.46, f32[32,128]{1,0:T(8,128)S(1)} %get-tuple-element.28.rows_ref, f32[128,128]{1,0:T(8,128)S(1)} %get-tuple-element.29.cols_ref, f32[32,512]{1,0:T(8,128)S(1)} %get-tuple-element.32.counts_ref, bf16[512,256]{1,0:T(8,128)(2,1)S(1)} %bitcast.39, ...), custom_call_target="tpu_custom_call" | custom-call | bytes 8388608 | tf_op jit(solution)/shard_map/ent_update/pallas_call | solution.py:54
  135.1 6.0 %all-to-all-done.5 = bf16[64,8,256]{2,1,0:T(8,128)(2,1)S(1)} async-done(((bf16[64,8,256]{2,1,0:T(8,128)(2,1)}), bf16[64,8,256]{2,1,0:T(8,128)(2,1)S(1)}, u32[]{:S(2)}, u32[]{:S(2)}) %all-to-all-start.5) | async-done | bytes 262176 | tf_op jit(solution)/shard_map/all_to_all | solution.py:401
  141.1 0.4 compact.3
  141.4 13.9 %all-gather.1 = bf16[2016,256]{1,0:T(8,128)(2,1)S(1)} all-gather(bf16[504,256]{1,0:T(8,128)(2,1)S(1)} %compact.3), channel_id=3, replica_groups=mesh['grp'=4,'wide'=64] {'grp'}, dimensions={0}, use_global_device_ids=true | all-gather | bytes 1290240 | tf_op jit(solution)/shard_map/all_gather | solution.py:520
  155.4 1.9 %word_final.1 = (f32[500,512]{1,0:T(8,128)}, f32[1,512]{1,0:T(1,128)}) custom-call(bf16[4,504,256]{2,1,0:T(8,128)(2,1)S(1)} %bitcast.32, f32[500,512]{1,0:T(8,128)S(1)} %get-tuple-element.41.table_ref, f32[1,512]{1,0:T(1,128)S(1)} %get-tuple-element.42.accum_ref), custom_call_target="tpu_custom_call" | custom-call | bytes 8388608 | tf_op jit(solution)/shard_map/word_final/pallas_call | solution.py:54
Async XLA Ops:
  2.9 13.0 %copy-start.7 = (s32[2,2,512]{2,1,0:T(2,128)S(1)}, s32[2,2,512]{2,1,0:T(2,128)}, u32[]{:S(2)}) copy-start(s32[2,2,512]{2,1,0:T(2,128)} %neg_hbm.1) | copy-start | bytes 24580
  2.9 22.2 %all-to-all-start = ((s32[64,1,128]{2,1,0:T(1,128)}), s32[64,1,128]{2,1,0:T(1,128)S(1)}, u32[]{:S(2)}, u32[]{:S(2)}) async-start(s32[64,1,128]{2,1,0:T(1,128)} %bitcast.5), calls=%async_computation | async-start | bytes 65536 | tf_op jit(solution)/shard_map/all_to_all | solution.py:401
  15.9 0.7 copy-start.9
  15.9 0.7 copy-start.8
  16.6 1.2 copy-start
  17.8 1.2 copy-start.2
  55.2 8.1 %copy-start.1 = (f32[512,500]{0,1:T(8,128)S(1)}, f32[512,500]{0,1:T(8,128)}, u32[]{:S(2)}) copy-start(f32[512,500]{0,1:T(8,128)} %param.15) | copy-start | bytes 3072004
  57.1 18.2 %all-to-all-start.2 = ((bf16[64,8,256]{2,1,0:T(8,128)(2,1)}), bf16[64,8,256]{2,1,0:T(8,128)(2,1)S(1)}, u32[]{:S(2)}, u32[]{:S(2)}) async-start(bf16[64,8,256]{2,1,0:T(8,128)(2,1)} %bitcast.13), calls=%async_computation.2 | async-start | bytes 524288 | tf_op jit(solution)/shard_map/all_to_all | solution.py:401
  68.0 1.0 copy-start.4
  68.9 0.8 copy-start.6
  75.3 23.4 %all-to-all-start.3 = ((bf16[64,8,512]{2,1,0:T(8,128)(2,1)}), bf16[64,8,512]{2,1,0:T(8,128)(2,1)S(1)}, u32[]{:S(2)}, u32[]{:S(2)}) async-start(bf16[64,8,512]{2,1,0:T(8,128)(2,1)} %bitcast.47), calls=%async_computation.3 | async-start | bytes 1048576 | tf_op jit(solution)/shard_map/all_to_all | solution.py:401
  81.4 14.0 %copy-start.3 = (f32[512,500]{0,1:T(8,128)S(1)}, f32[512,500]{0,1:T(8,128)}, u32[]{:S(2)}) copy-start(f32[512,500]{0,1:T(8,128)} %param.13) | copy-start | bytes 3072004
  123.0 18.0 %all-to-all-start.5 = ((bf16[64,8,256]{2,1,0:T(8,128)(2,1)}), bf16[64,8,256]{2,1,0:T(8,128)(2,1)S(1)}, u32[]{:S(2)}, u32[]{:S(2)}) async-start(bf16[64,8,256]{2,1,0:T(8,128)(2,1)} %bitcast.20), calls=%async_computation.5 | async-start | bytes 524288 | tf_op jit(solution)/shard_map/all_to_all | solution.py:401
  129.1 1.2 copy-start.5

commit v2 on v1

--- a/solution.py
+++ b/solution.py
@@ -46,7 +46,10 @@
 
 def kernel_call(body, out_shape, name, operands, scratch=(), hbm=(), hbm_out=(), moved=0, pin=False):
     if pin:
-        operands = [pltpu.with_memory_space_constraint(x, pltpu.HBM) for x in operands]
+        operands = [
+            pltpu.with_memory_space_constraint(x, pltpu.HBM) if i in hbm else x
+            for i, x in enumerate(operands)
+        ]
 
     def space(far):
         return pl.BlockSpec(memory_space=pltpu.HBM if far else pltpu.VMEM)
@@ -136,8 +139,11 @@
     neg_hbm,
     ent_sum_hbm,
     word_sum_hbm,
+    rows_ref,
+    cols_ref,
     ent_out,
     word_out,
+    pushed_out,
     counts_out,
     ent_sum_out,
     word_sum_out,
@@ -147,13 +153,27 @@
     scratch,
     sems,
 ):
-    fetch(
-        (neg_hbm, ent_hbm, word_hbm, ent_sum_hbm, word_sum_hbm),
-        (neg, ent, word, ent_sum_out, word_sum_out),
-        sems,
-    )
+    copies = [
+        pltpu.make_async_copy(source, target, sems.at[i])
+        for i, (source, target) in enumerate(
+            (
+                (ent_hbm, ent),
+                (word_hbm, word),
+                (neg_hbm, neg),
+                (ent_sum_hbm, ent_sum_out),
+                (word_sum_hbm, word_sum_out),
+            )
+        )
+    ]
+    for copy in copies:
+        copy.start()
+    copies[0].wait()
     to_half(ent, ent_out, scratch)
+    pushed_out[...] = pushed_sources(0, rows_ref, cols_ref, ent_out, pushed_out.shape[0])
+    copies[1].wait()
     to_half(word, word_out, scratch)
+    for copy in copies[2:]:
+        copy.wait()
     entity = iota((ent.shape[1], neg.shape[-1]), 0)
     ones = jnp.ones((8, neg.shape[-1]), BF16)
     for i in range(2 * STEPS):
@@ -211,22 +231,22 @@
     return named, nt(named, ent_half[...]).astype(BF16)
 
 
-def link_send(step, asks_ref, rows_ref, cols_ref, ent_half, out_ref, start):
-    ids = id_column(asks_ref, 2 * step + 1)
-    out_ref[:, start : start + HALF] = lookup(named_rows(ids, ent_half.shape[1]), ent_half)
+def pushed_sources(step, rows_ref, cols_ref, ent_half, rows):
     place = jnp.where(
         row_of(rows_ref, step, MASK_L) > 0.0, row_of(rows_ref, step, PLACE_L), -float(2 * CAP)
     )
     _, src = sources(step, cols_ref, ent_half)
-    out_ref[:, start + HALF : start + PAD] = put(
-        place, src[:, 0:HALF], src[:, HALF:PAD], out_ref.shape[0]
-    ).astype(BF16)
-
-
-def respond_body(asks_ref, rows_ref, cols_ref, word_half, ent_half, out_ref):
-    named = named_rows(id_column(asks_ref, 0), word_half.shape[1])
-    out_ref[:, 0:HALF] = lookup(named, word_half)
-    link_send(0, asks_ref, rows_ref, cols_ref, ent_half, out_ref, HALF)
+    return put(place, src[:, 0:HALF], src[:, HALF:PAD], rows).astype(BF16)
+
+
+def asked_rows(which, asks_ref, half_ref):
+    return lookup(named_rows(id_column(asks_ref, which), half_ref.shape[1]), half_ref)
+
+
+def respond_body(asks_ref, pushed_ref, word_half, ent_half, out_ref):
+    out_ref[:, 0:HALF] = asked_rows(0, asks_ref, word_half)
+    out_ref[:, HALF:PAD] = asked_rows(1, asks_ref, ent_half)
+    out_ref[:, PAD:] = pushed_ref[...]
 
 
 def take(recv, place):
@@ -334,34 +354,56 @@
     table_done.start()
     if not last:
         to_half(table, half_out, scratch)
-        link_send(step + 1, asks_ref, rows_ref, cols_ref, half_out, links_out, 0)
+        links_out[:, 0:HALF] = asked_rows(2 * step + 3, asks_ref, half_out)
+        links_out[:, HALF:] = pushed_sources(step + 1, rows_ref, cols_ref, half_out, rows)
     table_done.wait()
 
 
-def compact_body(recv_ref, out_ref):
+def compact_body(recv_ref, *outs):
     rows = recv_ref.shape[0]
-    places = out_ref.shape[1]
+    places = outs[0].shape[1]
     grads = jnp.transpose(recv_ref[...].astype(F32)).astype(BF16)
     row = lax.broadcasted_iota(jnp.int32, (rows, places), 0)
     place = lax.broadcasted_iota(jnp.int32, (rows, places), 1)
     place = place // CAP * (2 * CAP) + place % CAP
     low = nn(grads, hot(row == place))
     high = nn(grads, hot(row == place + CAP))
-    out_ref[...] = jnp.concatenate([low[0:CUT, :], high], axis=0).astype(BF16)
-
-
-def word_gradient(recv_ref, count):
-    groups, depth, places = recv_ref.shape
-    columns = jnp.concatenate([recv_ref[group] for group in range(groups)], axis=1)
+    columns = jnp.concatenate([low[0:CUT, :], high], axis=0).astype(BF16)
+    outs[0][...] = columns
+    for i, out in enumerate(outs[1:]):
+        half = out.shape[1]
+        out[...] = columns[:, i % 2 * half : (i % 2 + 1) * half]
+
+
+def word_gradient(columns, count):
+    depth, places = columns.shape
     ids = columns[depth - 8 :, :].astype(F32)
     ids = ids[4:5, :] * 16.0 + ids[5:6, :]
-    return nt(columns, hot(iota((count, groups * places), 0) == ids))
+    return nt(columns, hot(iota((count, places), 0) == ids))
+
+
+def joined(first_ref, second_ref):
+    return jnp.concatenate([first_ref[...], second_ref[...]], axis=1)
+
+
+def pair_gradient(mine_ref, far_low, far_high, count):
+    mine = word_gradient(mine_ref[...], count)
+    return mine + word_gradient(joined(far_low, far_high), count)
+
+
+def word_near_body(before_low, before_high, after_low, after_high, out_ref):
+    count = out_ref.shape[1]
+    before = word_gradient(joined(before_low, before_high), count)
+    out_ref[...] = before + word_gradient(joined(after_low, after_high), count)
 
 
 def word_update_body(
     step,
     asks_ref,
-    recv_ref,
+    mine_ref,
+    far_low,
+    far_high,
+    near_ref,
     table_hbm,
     accum_ref,
     table_out,
@@ -375,7 +417,7 @@
     table_in = pltpu.make_async_copy(table_hbm, table, sem)
     table_in.start()
     named = named_rows(id_column(asks_ref, 2 * step + 2), table.shape[1])
-    total = word_gradient(recv_ref, table.shape[1])
+    total = near_ref[...] + pair_gradient(mine_ref, far_low, far_high, table.shape[1])
     table_in.wait()
     accum_out[...] = adagrad(table, accum_ref[...], total[0:CUT, :], total[CUT:, :])
     table_done = pltpu.make_async_copy(table, table_out, sem)
@@ -385,9 +427,12 @@
     table_done.wait()
 
 
-def word_final_body(recv_ref, table_ref, accum_ref, table_out, accum_out):
+def word_final_body(
+    mine_ref, far_low, far_high, near_ref, table_ref, accum_ref, table_out, accum_out
+):
     width, words = table_ref.shape
-    grad = word_gradient(recv_ref, words)[0:width, :]
+    total = near_ref[...] + pair_gradient(mine_ref, far_low, far_high, words)
+    grad = total[0:width, :]
     accum = accum_ref[...] + jnp.sum(grad * grad, axis=0, keepdims=True) * (1.0 / width)
     accum_out[...] = accum
     table_out[...] = table_ref[...] - grad * (LEARN * lax.rsqrt(accum))
@@ -399,6 +444,11 @@
 
 def exchange(x):
     return lax.all_to_all(x, "wide", split_axis=0, concat_axis=0, tiled=True)
+
+
+def shifted(x, by):
+    size = lax.axis_size("grp")
+    return lax.ppermute(x, "grp", [(i, (i + by) % size) for i in range(size)])
 
 
 def on_device(
@@ -445,17 +495,18 @@
     )
     asked = exchange(asks[:, None, :])[:, 0, :]
     half_shape = shape(PAD, entities, dtype=BF16)
-    ent_half, word_half, counts, ent_sum, word_sum = kernel_call(
+    ent_half, word_half, pushed, counts, ent_sum, word_sum = kernel_call(
         halves_body,
         (
             half_shape,
             shape(PAD, words, dtype=BF16),
+            shape(message, HALF, dtype=BF16),
             shape(8 * 2 * STEPS, entities),
             shape(1, entities),
             shape(1, words),
         ),
         "halves",
-        (ent, word, neg_rows, ent_sum, word_sum),
+        (ent, word, neg_rows, ent_sum, word_sum, rows, cols),
         scratch=(
             pltpu.VMEM(ent.shape, F32),
             pltpu.VMEM(word.shape, F32),
@@ -465,6 +516,7 @@
         ),
         hbm=range(5),
         moved=2**22,
+        pin=True,
     )
     send_shape = shape(message, 3 * HALF, dtype=BF16)
     links_shape = shape(message, PAD, dtype=BF16)
@@ -472,7 +524,7 @@
         respond_body,
         (send_shape,),
         "respond",
-        (asked, rows, cols, word_half, ent_half),
+        (asked, pushed, word_half, ent_half),
         moved=2**22,
     )
     for step in range(STEPS):
@@ -510,20 +562,25 @@
             ent_half = out[2]
             received, links = lax.optimization_barrier((received, out[3]))
             link_recv, link_at = exchange(links), 0
-        (mine,) = kernel_call(
-            compact_body,
-            (shape(CUT + HALF, peers * CAP, dtype=BF16),),
-            "compact",
-            (received,),
-            moved=2**20,
+        columns = (shape(CUT + HALF, peers * CAP, dtype=BF16),)
+        columns += (shape(CUT + HALF, peers * CAP // 2, dtype=BF16),) * 4
+        mine = kernel_call(compact_body, columns, "compact", (received,), moved=2**20)
+        before_low, after_high = shifted(mine[1], 1), shifted(mine[4], -1)
+        before_high, after_low = shifted(mine[2], 1), shifted(mine[3], -1)
+        far_low, far_high = shifted(before_low, 1), shifted(after_high, -1)
+        (near,) = kernel_call(
+            word_near_body,
+            (shape(CUT + HALF, words),),
+            "word_near",
+            (before_low, before_high, after_low, after_high),
+            moved=2**21,
         )
-        every = lax.all_gather(mine, "grp", axis=0, tiled=False)
         if last:
             word, word_sum = kernel_call(
                 word_final_body,
                 (shape(width, words), shape(1, words)),
                 "word_final",
-                (every, word, word_sum),
+                (mine[0], far_low, far_high, near, word, word_sum),
                 moved=2**23,
             )
         else:
@@ -531,14 +588,14 @@
                 functools.partial(word_update_body, step),
                 (shape(width, words), shape(1, words), shape(message, HALF, dtype=BF16)),
                 "word_update",
-                (asked, every, word, word_sum),
+                (asked, mine[0], far_low, far_high, near, word, word_sum),
                 scratch=(
                     pltpu.VMEM((width, words), F32),
                     pltpu.VMEM((PAD, words), BF16),
                     pltpu.VMEM((PAD, words), F32),
                     pltpu.SemaphoreType.DMA,
                 ),
-                hbm=(2,),
+                hbm=(5,),
                 hbm_out=(0,),
                 moved=2**23,
             )

time: 159 us -> 153 us (0.962)
  blocking collectives: 78.6 us -> 65 us
  starting transfers between devices: 31.2 us -> 42 us
  local copies, waits for them, and re-layouts: 6.09 us -> 1.76 us
  waiting for transfers between devices: 17.3 us -> 19.2 us
    all_gather x2 -> x0, blocking collectives: 27.5 us -> none  [on_device(): every = lax.all_gather(mine, 'grp', axis=0, tiled=False)]
    ppermute x0 -> x12, starting transfers between devices: none -> 16.7 us  [shifted(): return lax.ppermute(x, 'grp', [(i, (i + by) % size) for i in range(size)])]
    all_to_all x2 -> x3, blocking collectives: 51 us -> 65 us  [exchange(): return lax.all_to_all(x, 'wide', split_axis=0, concat_axis=0, tiled=True)]
    all_to_all x4 -> x3, starting transfers between devices: 31.2 us -> 25.2 us  [exchange(): return lax.all_to_all(x, 'wide', split_axis=0, concat_axis=0, tiled=True)]
    unnamed x20 -> x10, local copies, waits for them, and re-layouts: 6.09 us -> 1.76 us
    ppermute x0 -> x12, waiting for transfers between devices: none -> 3.23 us  [shifted(): return lax.ppermute(x, 'grp', [(i, (i + by) % size) for i in range(size)])]
    all_to_all x4 -> x3, waiting for transfers between devices: 17.3 us -> 16 us  [exchange(): return lax.all_to_all(x, 'wide', split_axis=0, concat_axis=0, tiled=True)]
    pallas_call x11 -> x13, Pallas kernels: 23.3 us -> 23.6 us  [kernel_call(): pl.pallas_call(body, out_shape=out_shape, in_specs=[space(i in hbm) for i...]
  transfers between devices with their start and end apart: 4 -> 15, of which waited for: 4 -> 6; matrix products, arithmetic and copies ran while one was open for 0% -> 0% of each run, Pallas kernels for 9% -> 10%
where the time goes in v2:
time: 153 us; the launch traced here: 152 us
  blocking collectives  65 us (42%)
  starting transfers between devices  42 us (27%)
  Pallas kernels  23.6 us (15%)
  waiting for transfers between devices  19.2 us (13%)
  local copies, waits for them, and re-layouts  1.76 us (1%)
    all_to_all x3, blocking collectives, exchange(): return lax.all_to_all(x, 'wide', split_axis=0, concat_axis=0, tiled=True)  65 us
    all_to_all x3, starting transfers between devices, exchange(): return lax.all_to_all(x, 'wide', split_axis=0, concat_axis=0, tiled=True)  25.2 us
    pallas_call x13, Pallas kernels, kernel_call(): pl.pallas_call(body, out_shape=out_shape, in_specs=[space(i in hbm) for i...  23.6 us
    ppermute x12, starting transfers between devices, shifted(): return lax.ppermute(x, 'grp', [(i, (i + by) % size) for i in range(size)])  16.7 us
    all_to_all x3, waiting for transfers between devices, exchange(): return lax.all_to_all(x, 'wide', split_axis=0, concat_axis=0, tiled=True)  16 us
    ppermute x12, waiting for transfers between devices, shifted(): return lax.ppermute(x, 'grp', [(i, (i + by) % size) for i in range(size)])  3.23 us
  transfers between devices with their start and end apart: 15, of which 6 were waited for; matrix products, arithmetic and copies ran while one was open for 0% of the time, Pallas kernels for 10%

profile of v2, /device:TPU:1, one launch (start us, length us, event | category | flops | bytes accessed | tf_op | source)
XLA Modules:
  0.0 152.3 jit_solution(10820456999644806751)
XLA Ops:
  0.6 2.2 %prepare.1 = (s32[64,128]{1,0:T(8,128)}, f32[32,128]{1,0:T(8,128)S(1)}, f32[128,128]{1,0:T(8,128)S(1)}) custom-call(s32[2,128]{1,0:T(2,128)} %bitcast.48, s32[2,128]{1,0:T(2,128)} %bitcast.49, s32[2,128]{1,0:T(2,128)} %refs_2_.1, s32[2,128]{1,0:T(2,128)} %refs_3_.1, s32[2,128]{1,0:T(2,128)} %refs_4_.1, s32[2,128]{1,0:T(2,128)} %refs_5_.1, s32[1,2]{1,0:T(1,128)} %bitcast.50, ...), custom_call_target="tpu_custom_call" | custom-call | bytes 262144 | tf_op jit(solution)/shard_map/prepare/pallas_call | solution.py:57
  2.9 13.0 %all-to-all-start = ((s32[64,1,128]{2,1,0:T(1,128)}), s32[64,1,128]{2,1,0:T(1,128)S(1)}, u32[]{:S(2)}, u32[]{:S(2)}) async-start(s32[64,1,128]{2,1,0:T(1,128)} %bitcast.5), calls=%async_computation | async-start | bytes 65536 | tf_op jit(solution)/shard_map/all_to_all | solution.py:446
  15.9 2.5 %halves.1 = (bf16[512,512]{1,0:T(8,128)(2,1)S(1)}, bf16[512,512]{1,0:T(8,128)(2,1)S(1)}, bf16[512,256]{1,0:T(8,128)(2,1)S(1)}, f32[32,512]{1,0:T(8,128)S(1)}, f3...) custom-call(f32[500,512]{1,0:T(8,128)} %bitcast.29, f32[500,512]{1,0:T(8,128)} %bitcast.31, s32[2,2,512]{2,1,0:T(2,128)} %neg_hbm.1, ...), custom_call_target="tpu_custom_call" | custom-call | bytes 4194304 | tf_op jit(solution)/shard_map/halves/pallas_call | solution.py:57
  18.4 6.7 %all-to-all-done = s32[64,1,128]{2,1,0:T(1,128)S(1)} async-done(((s32[64,1,128]{2,1,0:T(1,128)}), s32[64,1,128]{2,1,0:T(1,128)S(1)}, u32[]{:S(2)}, u32[]{:S(2)}) %all-to-all-start) | async-done | bytes 32800 | tf_op jit(solution)/shard_map/all_to_all | solution.py:446
  25.1 1.1 respond.1
  26.2 27.0 %all_to_all.62 = bf16[64,8,768]{2,1,0:T(8,128)(2,1)S(1)} all-to-all(bf16[64,8,768]{2,1,0:T(8,128)(2,1)S(1)} %bitcast.33), channel_id=1, replica_groups=mesh['grp'=4,'wide'=64] {'wide'}, dimensions={0} | all-to-all | bytes 1572864 | tf_op jit(solution)/shard_map/all_to_all | solution.py:446
  53.2 0.0 copy-start
  53.2 1.9 %anchor.2 = bf16[512,256]{1,0:T(8,128)(2,1)} custom-call(bf16[512,768]{1,0:T(8,128)(2,1)S(1)} %bitcast.26, f32[32,128]{1,0:T(8,128)S(1)} %get-tuple-element.39.rows_ref, f32[128,128]{1,0:T(8,128)S(1)} %get-tuple-element.40.cols_ref, f32[32,512]{1,0:T(8,128)S(1)} %get-tuple-element.44.counts_ref, bf16[512,512]{1,0:T(8,128)(2,1)S(1)} %get-tuple-element.43.ent_half), custom_call_target="tpu_custom_call" | custom-call | bytes 4194304 | tf_op jit(solution)/shard_map/anchor/pallas_call | solution.py:57
  55.1 6.2 %all-to-all-start.2 = ((bf16[64,8,256]{2,1,0:T(8,128)(2,1)}), bf16[64,8,256]{2,1,0:T(8,128)(2,1)S(1)}, u32[]{:S(2)}, u32[]{:S(2)}) async-start(bf16[64,8,256]{2,1,0:T(8,128)(2,1)} %bitcast.13), calls=%async_computation.2 | async-start | bytes 524288 | tf_op jit(solution)/shard_map/all_to_all | solution.py:446
  61.3 0.0 copy-done
  61.4 4.6 %ent_update.2 = (f32[500,512]{1,0:T(8,128)S(1)}, f32[1,512]{1,0:T(1,128)S(1)}, bf16[512,512]{1,0:T(8,128)(2,1)S(1)}, bf16[512,512]{1,0:T(8,128)(2,1)S(1)}) custom-call(s32[64,128]{1,0:T(8,128)S(1)} %bitcast.41, f32[32,128]{1,0:T(8,128)S(1)} %get-tuple-element.39.rows_ref, f32[128,128]{1,0:T(8,128)S(1)} %get-tuple-element.40.cols_ref, ...), custom_call_target="tpu_custom_call" | custom-call | bytes 8388608 | tf_op jit(solution)/shard_map/ent_update/pallas_call | solution.py:57
  66.0 0.0 copy-start.2
  66.0 1.0 copy-done.2
  66.9 0.0 copy-start.4
  66.9 0.8 copy-done.4
  67.7 5.6 %all-to-all-done.2 = bf16[64,8,256]{2,1,0:T(8,128)(2,1)S(1)} async-done(((bf16[64,8,256]{2,1,0:T(8,128)(2,1)}), bf16[64,8,256]{2,1,0:T(8,128)(2,1)S(1)}, u32[]{:S(2)}, u32[]{:S(2)}) %all-to-all-start.2) | async-done | bytes 262176 | tf_op jit(solution)/shard_map/all_to_all | solution.py:446
  73.3 6.0 %all-to-all-start.3 = ((bf16[64,8,512]{2,1,0:T(8,128)(2,1)}), bf16[64,8,512]{2,1,0:T(8,128)(2,1)S(1)}, u32[]{:S(2)}, u32[]{:S(2)}) async-start(bf16[64,8,512]{2,1,0:T(8,128)(2,1)} %bitcast.44), calls=%async_computation.3 | async-start | bytes 1048576 | tf_op jit(solution)/shard_map/all_to_all | solution.py:446
  79.4 0.0 copy-start.1
  79.4 0.4 compact.2
  79.8 1.4 collective-permute-start
  81.1 1.5 collective-permute-start.2
  82.7 0.0 collective-permute-start.4
  82.7 2.7 %collective-permute-start.5 = (bf16[504,128]{1,0:T(8,128)(2,1)S(1)}, bf16[504,128]{1,0:T(8,128)(2,1)S(1)}, u32[]{:S(2)}, u32[]{:S(2)}) collective-permute-start(bf16[504,128]{1,0:T(8,128)(2,1)S(1)} %get-tuple-element.52), channel_id=1, source_target_pairs={{0,192},{64,0},{128,64},{192,128},{1,193},{65,1},{129,65},{193,129... | collective-permute-start | bytes 387080 | tf_op jit(solution)/shard_map/ppermute | solution.py:451
  85.3 0.4 collective-permute-done.before_low
  85.8 0.0 collective-permute-start.1
  85.8 0.0 collective-permute-done.2.after_high
  85.8 2.7 %collective-permute-start.3 = (bf16[504,128]{1,0:T(8,128)(2,1)S(1)}, bf16[504,128]{1,0:T(8,128)(2,1)S(1)}, u32[]{:S(2)}, u32[]{:S(2)}) collective-permute-start(bf16[504,128]{1,0:T(8,128)(2,1)S(1)} %collective-permute-done.2.after_high), channel_id=1, source_target_pairs={{0,192},{64,0},{128,64},{192,128},{1,193},{65,1},{129,65},{193,129... | collective-permute-start | bytes 387080 | tf_op jit(solution)/shard_map/ppermute | solution.py:451
  88.4 0.0 collective-permute-done.4.before_high
  88.4 0.0 collective-permute-done.5.after_low
  88.4 0.5 word_near.2.near_ref
  88.9 2.1 %collective-permute-done.1.far_low = bf16[504,128]{1,0:T(8,128)(2,1)S(1)} collective-permute-done((bf16[504,128]{1,0:T(8,128)(2,1)S(1)}, bf16[504,128]{1,0:T(8,128)(2,1)S(1)}, u32[]{:S(2)}, u32[]{:S(2)}) %collective-permute-start.1) | collective-permute-done | bytes 129056 | tf_op jit(solution)/shard_map/ppermute | solution.py:451
  91.1 0.0 collective-permute-done.3.far_high
  91.1 0.0 copy-done.1
  91.1 1.9 %word_update.1 = (f32[500,512]{1,0:T(8,128)S(1)}, f32[1,512]{1,0:T(1,128)S(1)}, bf16[512,256]{1,0:T(8,128)(2,1)S(1)}) custom-call(s32[64,128]{1,0:T(8,128)S(1)} %bitcast.42, bf16[504,256]{1,0:T(8,128)(2,1)S(1)} %get-tuple-element.48.mine_ref, bf16[504,128]{1,0:T(8,128)(2,1)S(1)} %collective-permute-done.1.far_low, ...), custom_call_target="tpu_custom_call" | custom-call | bytes 8388608 | tf_op jit(solution)/shard_map/word_update/pallas_call | solution.py:57
  93.0 3.7 %all-to-all-done.3 = bf16[64,8,512]{2,1,0:T(8,128)(2,1)S(1)} async-done(((bf16[64,8,512]{2,1,0:T(8,128)(2,1)}), bf16[64,8,512]{2,1,0:T(8,128)(2,1)S(1)}, u32[]{:S(2)}, u32[]{:S(2)}) %all-to-all-start.3) | async-done | bytes 524320 | tf_op jit(solution)/shard_map/all_to_all | solution.py:446
  96.7 20.1 %all_to_all.63 = bf16[64,8,256]{2,1,0:T(8,128)(2,1)S(1)} all-to-all(bf16[64,8,256]{2,1,0:T(8,128)(2,1)S(1)} %bitcast.45), channel_id=1, replica_groups=mesh['grp'=4,'wide'=64] {'wide'}, dimensions={0} | all-to-all | bytes 524288 | tf_op jit(solution)/shard_map/all_to_all | solution.py:446
  116.8 0.0 copy-start.3
  116.8 1.2 anchor.3
  118.0 17.8 %all_to_all.64 = bf16[64,8,256]{2,1,0:T(8,128)(2,1)S(1)} all-to-all(bf16[64,8,256]{2,1,0:T(8,128)(2,1)S(1)} %bitcast.39), channel_id=1, replica_groups=mesh['grp'=4,'wide'=64] {'wide'}, dimensions={0} | all-to-all | bytes 524288 | tf_op jit(solution)/shard_map/all_to_all | solution.py:446
  135.9 0.4 compact.3
  136.2 1.3 collective-permute-start.6
  137.5 1.8 %collective-permute-start.8 = (bf16[504,128]{1,0:T(8,128)(2,1)S(1)}, bf16[504,128]{1,0:T(8,128)(2,1)S(1)}, u32[]{:S(2)}, u32[]{:S(2)}) collective-permute-start(bf16[504,128]{1,0:T(8,128)(2,1)S(1)} %get-tuple-element.60), channel_id=1, source_target_pairs={{0,192},{64,0},{128,64},{192,128},{1,193},{65,1},{129,65},{193,129... | collective-permute-start | bytes 387080 | tf_op jit(solution)/shard_map/ppermute | solution.py:451
  139.4 0.0 collective-permute-start.10
  139.4 2.7 %collective-permute-start.11 = (bf16[504,128]{1,0:T(8,128)(2,1)S(1)}, bf16[504,128]{1,0:T(8,128)(2,1)S(1)}, u32[]{:S(2)}, u32[]{:S(2)}) collective-permute-start(bf16[504,128]{1,0:T(8,128)(2,1)S(1)} %get-tuple-element.62), channel_id=1, source_target_pairs={{0,192},{64,0},{128,64},{192,128},{1,193},{65,1},{129,65},{193,129... | collective-permute-start | bytes 387080 | tf_op jit(solution)/shard_map/ppermute | solution.py:451
  142.0 0.7 collective-permute-done.6.before_low
  142.7 0.0 collective-permute-start.7
  142.7 0.0 collective-permute-done.8.after_high
  142.7 2.7 %collective-permute-start.9 = (bf16[504,128]{1,0:T(8,128)(2,1)S(1)}, bf16[504,128]{1,0:T(8,128)(2,1)S(1)}, u32[]{:S(2)}, u32[]{:S(2)}) collective-permute-start(bf16[504,128]{1,0:T(8,128)(2,1)S(1)} %collective-permute-done.8.after_high), channel_id=1, source_target_pairs={{0,192},{64,0},{128,64},{192,128},{1,193},{65,1},{129,65},{193,129... | collective-permute-start | bytes 387080 | tf_op jit(solution)/shard_map/ppermute | solution.py:451
  145.4 0.0 copy-done.3
  145.4 4.8 %ent_update.3 = (f32[500,512]{1,0:T(8,128)}, f32[1,512]{1,0:T(1,128)}) custom-call(s32[64,128]{1,0:T(8,128)S(1)} %bitcast.43, f32[32,128]{1,0:T(8,128)S(1)} %get-tuple-element.39.rows_ref, f32[128,128]{1,0:T(8,128)S(1)} %get-tuple-element.40.cols_ref, f32[32,512]{1,0:T(8,128)S(1)} %get-tuple-element.44.counts_ref, bf16[512,256]{1,0:T(8,128)(2,1)S(1)} %bitcast.35, ...), custom_call_target="tpu_custom_call" | custom-call | bytes 8388608 | tf_op jit(solution)/shard_map/ent_update/pallas_call | solution.py:57
  150.2 0.0 collective-permute-done.10.before_high
  150.2 0.0 collective-permute-done.11.after_low
  150.2 0.5 word_near.3.near_ref
  150.7 0.0 collective-permute-done.7.far_low
  150.7 0.0 collective-permute-done.9.far_high
  150.7 1.6 %word_final.1 = (f32[500,512]{1,0:T(8,128)}, f32[1,512]{1,0:T(1,128)}) custom-call(bf16[504,256]{1,0:T(8,128)(2,1)S(1)} %get-tuple-element.58.mine_ref, bf16[504,128]{1,0:T(8,128)(2,1)S(1)} %collective-permute-done.7.far_low, bf16[504,128]{1,0:T(8,128)(2,1)S(1)} %collective-permute-done.9.far_high, f32[504,512]{1,0:T(8,128)S(1)} %word_near.3.near_ref, ...), custom_call_target="tpu_custom_call" | custom-call | bytes 8388608 | tf_op jit(solution)/shard_map/word_final/pallas_call | solution.py:57
Async XLA Ops:
  2.9 22.2 %all-to-all-start = ((s32[64,1,128]{2,1,0:T(1,128)}), s32[64,1,128]{2,1,0:T(1,128)S(1)}, u32[]{:S(2)}, u32[]{:S(2)}) async-start(s32[64,1,128]{2,1,0:T(1,128)} %bitcast.5), calls=%async_computation | async-start | bytes 65536 | tf_op jit(solution)/shard_map/all_to_all | solution.py:446
  53.2 8.1 %copy-start = (f32[512,500]{0,1:T(8,128)S(1)}, f32[512,500]{0,1:T(8,128)}, u32[]{:S(2)}) copy-start(f32[512,500]{0,1:T(8,128)} %param.15) | copy-start | bytes 3072004
  55.1 18.2 %all-to-all-start.2 = ((bf16[64,8,256]{2,1,0:T(8,128)(2,1)}), bf16[64,8,256]{2,1,0:T(8,128)(2,1)S(1)}, u32[]{:S(2)}, u32[]{:S(2)}) async-start(bf16[64,8,256]{2,1,0:T(8,128)(2,1)} %bitcast.13), calls=%async_computation.2 | async-start | bytes 524288 | tf_op jit(solution)/shard_map/all_to_all | solution.py:446
  66.0 1.0 copy-start.2
  66.9 0.8 copy-start.4
  73.3 23.4 %all-to-all-start.3 = ((bf16[64,8,512]{2,1,0:T(8,128)(2,1)}), bf16[64,8,512]{2,1,0:T(8,128)(2,1)S(1)}, u32[]{:S(2)}, u32[]{:S(2)}) async-start(bf16[64,8,512]{2,1,0:T(8,128)(2,1)} %bitcast.44), calls=%async_computation.3 | async-start | bytes 1048576 | tf_op jit(solution)/shard_map/all_to_all | solution.py:446
  79.4 11.7 %copy-start.1 = (f32[512,500]{0,1:T(8,128)S(1)}, f32[512,500]{0,1:T(8,128)}, u32[]{:S(2)}) copy-start(f32[512,500]{0,1:T(8,128)} %param.13) | copy-start | bytes 3072004
  79.8 6.0 %collective-permute-start = (bf16[504,128]{1,0:T(8,128)(2,1)S(1)}, bf16[504,128]{1,0:T(8,128)(2,1)S(1)}, u32[]{:S(2)}, u32[]{:S(2)}) collective-permute-start(bf16[504,128]{1,0:T(8,128)(2,1)S(1)} %get-tuple-element.49), channel_id=1, source_target_pairs={{0,64},{64,128},{128,192},{192,0},{1,65},{65,129},{129,193},{193,1... | collective-permute-start | bytes 387080 | tf_op jit(solution)/shard_map/ppermute | solution.py:451
  81.1 4.6 %collective-permute-start.2 = (bf16[504,128]{1,0:T(8,128)(2,1)S(1)}, bf16[504,128]{1,0:T(8,128)(2,1)S(1)}, u32[]{:S(2)}, u32[]{:S(2)}) collective-permute-start(bf16[504,128]{1,0:T(8,128)(2,1)S(1)} %get-tuple-element.50), channel_id=1, source_target_pairs={{0,192},{64,0},{128,64},{192,128},{1,193},{65,1},{129,65},{193,129... | collective-permute-start | bytes 387080 | tf_op jit(solution)/shard_map/ppermute | solution.py:451
  82.7 5.8 %collective-permute-start.4 = (bf16[504,128]{1,0:T(8,128)(2,1)S(1)}, bf16[504,128]{1,0:T(8,128)(2,1)S(1)}, u32[]{:S(2)}, u32[]{:S(2)}) collective-permute-start(bf16[504,128]{1,0:T(8,128)(2,1)S(1)} %get-tuple-element.51), channel_id=1, source_target_pairs={{0,64},{64,128},{128,192},{192,0},{1,65},{65,129},{129,193},{193,1... | collective-permute-start | bytes 387080 | tf_op jit(solution)/shard_map/ppermute | solution.py:451
  82.7 5.8 %collective-permute-start.5 = (bf16[504,128]{1,0:T(8,128)(2,1)S(1)}, bf16[504,128]{1,0:T(8,128)(2,1)S(1)}, u32[]{:S(2)}, u32[]{:S(2)}) collective-permute-start(bf16[504,128]{1,0:T(8,128)(2,1)S(1)} %get-tuple-element.52), channel_id=1, source_target_pairs={{0,192},{64,0},{128,64},{192,128},{1,193},{65,1},{129,65},{193,129... | collective-permute-start | bytes 387080 | tf_op jit(solution)/shard_map/ppermute | solution.py:451
  85.8 5.3 %collective-permute-start.1 = (bf16[504,128]{1,0:T(8,128)(2,1)S(1)}, bf16[504,128]{1,0:T(8,128)(2,1)S(1)}, u32[]{:S(2)}, u32[]{:S(2)}) collective-permute-start(bf16[504,128]{1,0:T(8,128)(2,1)S(1)} %collective-permute-done.before_low), channel_id=1, source_target_pairs={{0,64},{64,128},{128,192},{192,0},{1,65},{65,129},{129,193},{193,1... | collective-permute-start | bytes 387080 | tf_op jit(solution)/shard_map/ppermute | solution.py:451
  85.8 5.3 %collective-permute-start.3 = (bf16[504,128]{1,0:T(8,128)(2,1)S(1)}, bf16[504,128]{1,0:T(8,128)(2,1)S(1)}, u32[]{:S(2)}, u32[]{:S(2)}) collective-permute-start(bf16[504,128]{1,0:T(8,128)(2,1)S(1)} %collective-permute-done.2.after_high), channel_id=1, source_target_pairs={{0,192},{64,0},{128,64},{192,128},{1,193},{65,1},{129,65},{193,129... | collective-permute-start | bytes 387080 | tf_op jit(solution)/shard_map/ppermute | solution.py:451
  116.8 28.6 %copy-start.3 = (f32[500,512]{1,0:T(8,128)S(1)}, f32[500,512]{1,0:T(8,128)}, u32[]{:S(2)}) copy-start(f32[500,512]{1,0:T(8,128)} %copy-done.2) | copy-start | bytes 3072004
  136.2 6.5 %collective-permute-start.6 = (bf16[504,128]{1,0:T(8,128)(2,1)S(1)}, bf16[504,128]{1,0:T(8,128)(2,1)S(1)}, u32[]{:S(2)}, u32[]{:S(2)}) collective-permute-start(bf16[504,128]{1,0:T(8,128)(2,1)S(1)} %get-tuple-element.59), channel_id=1, source_target_pairs={{0,64},{64,128},{128,192},{192,0},{1,65},{65,129},{129,193},{193,1... | collective-permute-start | bytes 387080 | tf_op jit(solution)/shard_map/ppermute | solution.py:451
  137.5 5.2 %collective-permute-start.8 = (bf16[504,128]{1,0:T(8,128)(2,1)S(1)}, bf16[504,128]{1,0:T(8,128)(2,1)S(1)}, u32[]{:S(2)}, u32[]{:S(2)}) collective-permute-start(bf16[504,128]{1,0:T(8,128)(2,1)S(1)} %get-tuple-element.60), channel_id=1, source_target_pairs={{0,192},{64,0},{128,64},{192,128},{1,193},{65,1},{129,65},{193,129... | collective-permute-start | bytes 387080 | tf_op jit(solution)/shard_map/ppermute | solution.py:451
  139.4 10.8 %collective-permute-start.10 = (bf16[504,128]{1,0:T(8,128)(2,1)S(1)}, bf16[504,128]{1,0:T(8,128)(2,1)S(1)}, u32[]{:S(2)}, u32[]{:S(2)}) collective-permute-start(bf16[504,128]{1,0:T(8,128)(2,1)S(1)} %get-tuple-element.61), channel_id=1, source_target_pairs={{0,64},{64,128},{128,192},{192,0},{1,65},{65,129},{129,193},{193,1... | collective-permute-start | bytes 387080 | tf_op jit(solution)/shard_map/ppermute | solution.py:451
  139.4 10.8 %collective-permute-start.11 = (bf16[504,128]{1,0:T(8,128)(2,1)S(1)}, bf16[504,128]{1,0:T(8,128)(2,1)S(1)}, u32[]{:S(2)}, u32[]{:S(2)}) collective-permute-start(bf16[504,128]{1,0:T(8,128)(2,1)S(1)} %get-tuple-element.62), channel_id=1, source_target_pairs={{0,192},{64,0},{128,64},{192,128},{1,193},{65,1},{129,65},{193,129... | collective-permute-start | bytes 387080 | tf_op jit(solution)/shard_map/ppermute | solution.py:451
  142.7 8.0 %collective-permute-start.7 = (bf16[504,128]{1,0:T(8,128)(2,1)S(1)}, bf16[504,128]{1,0:T(8,128)(2,1)S(1)}, u32[]{:S(2)}, u32[]{:S(2)}) collective-permute-start(bf16[504,128]{1,0:T(8,128)(2,1)S(1)} %collective-permute-done.6.before_low), channel_id=1, source_target_pairs={{0,64},{64,128},{128,192},{192,0},{1,65},{65,129},{129,193},{193,1... | collective-permute-start | bytes 387080 | tf_op jit(solution)/shard_map/ppermute | solution.py:451
  142.7 8.0 %collective-permute-start.9 = (bf16[504,128]{1,0:T(8,128)(2,1)S(1)}, bf16[504,128]{1,0:T(8,128)(2,1)S(1)}, u32[]{:S(2)}, u32[]{:S(2)}) collective-permute-start(bf16[504,128]{1,0:T(8,128)(2,1)S(1)} %collective-permute-done.8.after_high), channel_id=1, source_target_pairs={{0,192},{64,0},{128,64},{192,128},{1,193},{65,1},{129,65},{193,129... | collective-permute-start | bytes 387080 | tf_op jit(solution)/shard_map/ppermute | solution.py:451

commit v3 on v2

--- a/solution.py
+++ b/solution.py
@@ -428,14 +428,23 @@
 
 
 def word_final_body(
-    mine_ref, far_low, far_high, near_ref, table_ref, accum_ref, table_out, accum_out
+    mine_ref, far_low, far_high, near_ref, table_ref, accum_ref, table_out, accum_out, table, sems
 ):
     width, words = table_ref.shape
     total = near_ref[...] + pair_gradient(mine_ref, far_low, far_high, words)
     grad = total[0:width, :]
     accum = accum_ref[...] + jnp.sum(grad * grad, axis=0, keepdims=True) * (1.0 / width)
     accum_out[...] = accum
-    table_out[...] = table_ref[...] - grad * (LEARN * lax.rsqrt(accum))
+    rate = LEARN * lax.rsqrt(accum)
+    copies = []
+    for i, (start, end) in enumerate(((0, HALF), (HALF, width))):
+        table[start:end, :] = table_ref[start:end, :] - grad[start:end, :] * rate
+        copies.append(
+            pltpu.make_async_copy(table.at[start:end], table_out.at[start:end], sems.at[i])
+        )
+        copies[i].start()
+    for copy in copies:
+        copy.wait()
 
 
 def shape(*dims, dtype=F32):
@@ -581,6 +590,8 @@
                 (shape(width, words), shape(1, words)),
                 "word_final",
                 (mine[0], far_low, far_high, near, word, word_sum),
+                scratch=(pltpu.VMEM((width, words), F32), pltpu.SemaphoreType.DMA((2,))),
+                hbm_out=(0,),
                 moved=2**23,
             )
         else:

time: 153 us -> 153 us (level)
  no operation moved by 1% of the time
where the time goes in v3:
time: 153 us
  blocking collectives  65 us (42%)
  starting transfers between devices  42 us (27%)
  Pallas kernels  24.2 us (16%)
  waiting for transfers between devices  19.2 us (13%)
  local copies, waits for them, and re-layouts  1.76 us (1%)
    all_to_all x3, blocking collectives, exchange(): return lax.all_to_all(x, 'wide', split_axis=0, concat_axis=0, tiled=True)  65 us
    all_to_all x3, starting transfers between devices, exchange(): return lax.all_to_all(x, 'wide', split_axis=0, concat_axis=0, tiled=True)  25.2 us
    pallas_call x13, Pallas kernels, kernel_call(): pl.pallas_call(body, out_shape=out_shape, in_specs=[space(i in hbm) for i...  24.2 us
    ppermute x12, starting transfers between devices, shifted(): return lax.ppermute(x, 'grp', [(i, (i + by) % size) for i in range(size)])  16.7 us
    all_to_all x3, waiting for transfers between devices, exchange(): return lax.all_to_all(x, 'wide', split_axis=0, concat_axis=0, tiled=True)  16 us
    ppermute x12, waiting for transfers between devices, shifted(): return lax.ppermute(x, 'grp', [(i, (i + by) % size) for i in range(size)])  3.23 us
  transfers between devices with their start and end apart: 15, of which 6 were waited for; matrix products, arithmetic and copies ran while one was open for 0% of the time, Pallas kernels for 10%

profile of v3, /device:TPU:1, one launch (start us, length us, event | category | flops | bytes accessed | tf_op | source)
XLA Modules:
  0.0 153.1 jit_solution(18297622984892879101)
XLA Ops:
  0.6 2.2 %prepare.1 = (s32[64,128]{1,0:T(8,128)}, f32[32,128]{1,0:T(8,128)S(1)}, f32[128,128]{1,0:T(8,128)S(1)}) custom-call(s32[2,128]{1,0:T(2,128)} %bitcast.48, s32[2,128]{1,0:T(2,128)} %bitcast.49, s32[2,128]{1,0:T(2,128)} %refs_2_.1, s32[2,128]{1,0:T(2,128)} %refs_3_.1, s32[2,128]{1,0:T(2,128)} %refs_4_.1, s32[2,128]{1,0:T(2,128)} %refs_5_.1, s32[1,2]{1,0:T(1,128)} %bitcast.50, ...), custom_call_target="tpu_custom_call" | custom-call | bytes 262144 | tf_op jit(solution)/shard_map/prepare/pallas_call | solution.py:57
  2.9 13.0 %all-to-all-start = ((s32[64,1,128]{2,1,0:T(1,128)}), s32[64,1,128]{2,1,0:T(1,128)S(1)}, u32[]{:S(2)}, u32[]{:S(2)}) async-start(s32[64,1,128]{2,1,0:T(1,128)} %bitcast.5), calls=%async_computation | async-start | bytes 65536 | tf_op jit(solution)/shard_map/all_to_all | solution.py:455
  15.9 2.5 %halves.1 = (bf16[512,512]{1,0:T(8,128)(2,1)S(1)}, bf16[512,512]{1,0:T(8,128)(2,1)S(1)}, bf16[512,256]{1,0:T(8,128)(2,1)S(1)}, f32[32,512]{1,0:T(8,128)S(1)}, f3...) custom-call(f32[500,512]{1,0:T(8,128)} %bitcast.29, f32[500,512]{1,0:T(8,128)} %bitcast.31, s32[2,2,512]{2,1,0:T(2,128)} %neg_hbm.1, ...), custom_call_target="tpu_custom_call" | custom-call | bytes 4194304 | tf_op jit(solution)/shard_map/halves/pallas_call | solution.py:57
  18.4 6.7 %all-to-all-done = s32[64,1,128]{2,1,0:T(1,128)S(1)} async-done(((s32[64,1,128]{2,1,0:T(1,128)}), s32[64,1,128]{2,1,0:T(1,128)S(1)}, u32[]{:S(2)}, u32[]{:S(2)}) %all-to-all-start) | async-done | bytes 32800 | tf_op jit(solution)/shard_map/all_to_all | solution.py:455
  25.1 1.1 respond.1
  26.2 27.0 %all_to_all.62 = bf16[64,8,768]{2,1,0:T(8,128)(2,1)S(1)} all-to-all(bf16[64,8,768]{2,1,0:T(8,128)(2,1)S(1)} %bitcast.33), channel_id=1, replica_groups=mesh['grp'=4,'wide'=64] {'wide'}, dimensions={0} | all-to-all | bytes 1572864 | tf_op jit(solution)/shard_map/all_to_all | solution.py:455
  53.2 0.0 copy-start
  53.2 1.9 %anchor.2 = bf16[512,256]{1,0:T(8,128)(2,1)} custom-call(bf16[512,768]{1,0:T(8,128)(2,1)S(1)} %bitcast.26, f32[32,128]{1,0:T(8,128)S(1)} %get-tuple-element.39.rows_ref, f32[128,128]{1,0:T(8,128)S(1)} %get-tuple-element.40.cols_ref, f32[32,512]{1,0:T(8,128)S(1)} %get-tuple-element.44.counts_ref, bf16[512,512]{1,0:T(8,128)(2,1)S(1)} %get-tuple-element.43.ent_half), custom_call_target="tpu_custom_call" | custom-call | bytes 4194304 | tf_op jit(solution)/shard_map/anchor/pallas_call | solution.py:57
  55.1 6.2 %all-to-all-start.2 = ((bf16[64,8,256]{2,1,0:T(8,128)(2,1)}), bf16[64,8,256]{2,1,0:T(8,128)(2,1)S(1)}, u32[]{:S(2)}, u32[]{:S(2)}) async-start(bf16[64,8,256]{2,1,0:T(8,128)(2,1)} %bitcast.13), calls=%async_computation.2 | async-start | bytes 524288 | tf_op jit(solution)/shard_map/all_to_all | solution.py:455
  61.3 0.0 copy-done
  61.4 4.6 %ent_update.2 = (f32[500,512]{1,0:T(8,128)S(1)}, f32[1,512]{1,0:T(1,128)S(1)}, bf16[512,512]{1,0:T(8,128)(2,1)S(1)}, bf16[512,512]{1,0:T(8,128)(2,1)S(1)}) custom-call(s32[64,128]{1,0:T(8,128)S(1)} %bitcast.41, f32[32,128]{1,0:T(8,128)S(1)} %get-tuple-element.39.rows_ref, f32[128,128]{1,0:T(8,128)S(1)} %get-tuple-element.40.cols_ref, ...), custom_call_target="tpu_custom_call" | custom-call | bytes 8388608 | tf_op jit(solution)/shard_map/ent_update/pallas_call | solution.py:57
  66.0 0.0 copy-start.2
  66.0 1.0 copy-done.2
  66.9 0.0 copy-start.4
  66.9 0.8 copy-done.4
  67.7 5.6 %all-to-all-done.2 = bf16[64,8,256]{2,1,0:T(8,128)(2,1)S(1)} async-done(((bf16[64,8,256]{2,1,0:T(8,128)(2,1)}), bf16[64,8,256]{2,1,0:T(8,128)(2,1)S(1)}, u32[]{:S(2)}, u32[]{:S(2)}) %all-to-all-start.2) | async-done | bytes 262176 | tf_op jit(solution)/shard_map/all_to_all | solution.py:455
  73.3 6.0 %all-to-all-start.3 = ((bf16[64,8,512]{2,1,0:T(8,128)(2,1)}), bf16[64,8,512]{2,1,0:T(8,128)(2,1)S(1)}, u32[]{:S(2)}, u32[]{:S(2)}) async-start(bf16[64,8,512]{2,1,0:T(8,128)(2,1)} %bitcast.44), calls=%async_computation.3 | async-start | bytes 1048576 | tf_op jit(solution)/shard_map/all_to_all | solution.py:455
  79.4 0.0 copy-start.1
  79.4 0.4 compact.2
  79.8 1.4 collective-permute-start
  81.1 1.5 collective-permute-start.2
  82.7 0.0 collective-permute-start.4
  82.7 2.7 %collective-permute-start.5 = (bf16[504,128]{1,0:T(8,128)(2,1)S(1)}, bf16[504,128]{1,0:T(8,128)(2,1)S(1)}, u32[]{:S(2)}, u32[]{:S(2)}) collective-permute-start(bf16[504,128]{1,0:T(8,128)(2,1)S(1)} %get-tuple-element.52), channel_id=1, source_target_pairs={{0,192},{64,0},{128,64},{192,128},{1,193},{65,1},{129,65},{193,129... | collective-permute-start | bytes 387080 | tf_op jit(solution)/shard_map/ppermute | solution.py:460
  85.3 0.4 collective-permute-done.before_low
  85.8 0.0 collective-permute-start.1
  85.8 0.0 collective-permute-done.2.after_high
  85.8 2.7 %collective-permute-start.3 = (bf16[504,128]{1,0:T(8,128)(2,1)S(1)}, bf16[504,128]{1,0:T(8,128)(2,1)S(1)}, u32[]{:S(2)}, u32[]{:S(2)}) collective-permute-start(bf16[504,128]{1,0:T(8,128)(2,1)S(1)} %collective-permute-done.2.after_high), channel_id=1, source_target_pairs={{0,192},{64,0},{128,64},{192,128},{1,193},{65,1},{129,65},{193,129... | collective-permute-start | bytes 387080 | tf_op jit(solution)/shard_map/ppermute | solution.py:460
  88.4 0.0 collective-permute-done.4.before_high
  88.4 0.0 collective-permute-done.5.after_low
  88.4 0.5 word_near.2.near_ref
  88.9 2.1 %collective-permute-done.1.far_low = bf16[504,128]{1,0:T(8,128)(2,1)S(1)} collective-permute-done((bf16[504,128]{1,0:T(8,128)(2,1)S(1)}, bf16[504,128]{1,0:T(8,128)(2,1)S(1)}, u32[]{:S(2)}, u32[]{:S(2)}) %collective-permute-start.1) | collective-permute-done | bytes 129056 | tf_op jit(solution)/shard_map/ppermute | solution.py:460
  91.1 0.0 collective-permute-done.3.far_high
  91.1 0.0 copy-done.1
  91.1 1.9 %word_update.1 = (f32[500,512]{1,0:T(8,128)S(1)}, f32[1,512]{1,0:T(1,128)S(1)}, bf16[512,256]{1,0:T(8,128)(2,1)S(1)}) custom-call(s32[64,128]{1,0:T(8,128)S(1)} %bitcast.42, bf16[504,256]{1,0:T(8,128)(2,1)S(1)} %get-tuple-element.48.mine_ref, bf16[504,128]{1,0:T(8,128)(2,1)S(1)} %collective-permute-done.1.far_low, ...), custom_call_target="tpu_custom_call" | custom-call | bytes 8388608 | tf_op jit(solution)/shard_map/word_update/pallas_call | solution.py:57
  93.0 3.7 %all-to-all-done.3 = bf16[64,8,512]{2,1,0:T(8,128)(2,1)S(1)} async-done(((bf16[64,8,512]{2,1,0:T(8,128)(2,1)}), bf16[64,8,512]{2,1,0:T(8,128)(2,1)S(1)}, u32[]{:S(2)}, u32[]{:S(2)}) %all-to-all-start.3) | async-done | bytes 524320 | tf_op jit(solution)/shard_map/all_to_all | solution.py:455
  96.7 20.1 %all_to_all.63 = bf16[64,8,256]{2,1,0:T(8,128)(2,1)S(1)} all-to-all(bf16[64,8,256]{2,1,0:T(8,128)(2,1)S(1)} %bitcast.45), channel_id=1, replica_groups=mesh['grp'=4,'wide'=64] {'wide'}, dimensions={0} | all-to-all | bytes 524288 | tf_op jit(solution)/shard_map/all_to_all | solution.py:455
  116.8 0.0 copy-start.3
  116.8 1.2 anchor.3
  118.0 17.8 %all_to_all.64 = bf16[64,8,256]{2,1,0:T(8,128)(2,1)S(1)} all-to-all(bf16[64,8,256]{2,1,0:T(8,128)(2,1)S(1)} %bitcast.39), channel_id=1, replica_groups=mesh['grp'=4,'wide'=64] {'wide'}, dimensions={0} | all-to-all | bytes 524288 | tf_op jit(solution)/shard_map/all_to_all | solution.py:455
  135.9 0.4 compact.3
  136.2 1.3 collective-permute-start.6
  137.5 1.8 %collective-permute-start.8 = (bf16[504,128]{1,0:T(8,128)(2,1)S(1)}, bf16[504,128]{1,0:T(8,128)(2,1)S(1)}, u32[]{:S(2)}, u32[]{:S(2)}) collective-permute-start(bf16[504,128]{1,0:T(8,128)(2,1)S(1)} %get-tuple-element.60), channel_id=1, source_target_pairs={{0,192},{64,0},{128,64},{192,128},{1,193},{65,1},{129,65},{193,129... | collective-permute-start | bytes 387080 | tf_op jit(solution)/shard_map/ppermute | solution.py:460
  139.4 0.0 collective-permute-start.10
  139.4 2.7 %collective-permute-start.11 = (bf16[504,128]{1,0:T(8,128)(2,1)S(1)}, bf16[504,128]{1,0:T(8,128)(2,1)S(1)}, u32[]{:S(2)}, u32[]{:S(2)}) collective-permute-start(bf16[504,128]{1,0:T(8,128)(2,1)S(1)} %get-tuple-element.62), channel_id=1, source_target_pairs={{0,192},{64,0},{128,64},{192,128},{1,193},{65,1},{129,65},{193,129... | collective-permute-start | bytes 387080 | tf_op jit(solution)/shard_map/ppermute | solution.py:460
  142.0 0.7 collective-permute-done.6.before_low
  142.7 0.0 collective-permute-start.7
  142.7 0.0 collective-permute-done.8.after_high
  142.7 2.7 %collective-permute-start.9 = (bf16[504,128]{1,0:T(8,128)(2,1)S(1)}, bf16[504,128]{1,0:T(8,128)(2,1)S(1)}, u32[]{:S(2)}, u32[]{:S(2)}) collective-permute-start(bf16[504,128]{1,0:T(8,128)(2,1)S(1)} %collective-permute-done.8.after_high), channel_id=1, source_target_pairs={{0,192},{64,0},{128,64},{192,128},{1,193},{65,1},{129,65},{193,129... | collective-permute-start | bytes 387080 | tf_op jit(solution)/shard_map/ppermute | solution.py:460
  145.4 0.0 copy-done.3
  145.4 4.8 %ent_update.3 = (f32[500,512]{1,0:T(8,128)}, f32[1,512]{1,0:T(1,128)}) custom-call(s32[64,128]{1,0:T(8,128)S(1)} %bitcast.43, f32[32,128]{1,0:T(8,128)S(1)} %get-tuple-element.39.rows_ref, f32[128,128]{1,0:T(8,128)S(1)} %get-tuple-element.40.cols_ref, f32[32,512]{1,0:T(8,128)S(1)} %get-tuple-element.44.counts_ref, bf16[512,256]{1,0:T(8,128)(2,1)S(1)} %bitcast.35, ...), custom_call_target="tpu_custom_call" | custom-call | bytes 8388608 | tf_op jit(solution)/shard_map/ent_update/pallas_call | solution.py:57
  150.2 0.0 collective-permute-done.10.before_high
  150.2 0.0 collective-permute-done.11.after_low
  150.2 0.5 word_near.3.near_ref
  150.7 0.0 collective-permute-done.7.far_low
  150.7 0.0 collective-permute-done.9.far_high
  150.7 2.2 %word_final.1 = (f32[500,512]{1,0:T(8,128)}, f32[1,512]{1,0:T(1,128)}) custom-call(bf16[504,256]{1,0:T(8,128)(2,1)S(1)} %get-tuple-element.58.mine_ref, bf16[504,128]{1,0:T(8,128)(2,1)S(1)} %collective-permute-done.7.far_low, bf16[504,128]{1,0:T(8,128)(2,1)S(1)} %collective-permute-done.9.far_high, f32[504,512]{1,0:T(8,128)S(1)} %word_near.3.near_ref, ...), custom_call_target="tpu_custom_call" | custom-call | bytes 8388608 | tf_op jit(solution)/shard_map/word_final/pallas_call | solution.py:57
Async XLA Ops:
  2.9 22.2 %all-to-all-start = ((s32[64,1,128]{2,1,0:T(1,128)}), s32[64,1,128]{2,1,0:T(1,128)S(1)}, u32[]{:S(2)}, u32[]{:S(2)}) async-start(s32[64,1,128]{2,1,0:T(1,128)} %bitcast.5), calls=%async_computation | async-start | bytes 65536 | tf_op jit(solution)/shard_map/all_to_all | solution.py:455
  53.2 8.1 %copy-start = (f32[512,500]{0,1:T(8,128)S(1)}, f32[512,500]{0,1:T(8,128)}, u32[]{:S(2)}) copy-start(f32[512,500]{0,1:T(8,128)} %param.15) | copy-start | bytes 3072004
  55.1 18.2 %all-to-all-start.2 = ((bf16[64,8,256]{2,1,0:T(8,128)(2,1)}), bf16[64,8,256]{2,1,0:T(8,128)(2,1)S(1)}, u32[]{:S(2)}, u32[]{:S(2)}) async-start(bf16[64,8,256]{2,1,0:T(8,128)(2,1)} %bitcast.13), calls=%async_computation.2 | async-start | bytes 524288 | tf_op jit(solution)/shard_map/all_to_all | solution.py:455
  66.0 1.0 copy-start.2
  66.9 0.8 copy-start.4
  73.3 23.4 %all-to-all-start.3 = ((bf16[64,8,512]{2,1,0:T(8,128)(2,1)}), bf16[64,8,512]{2,1,0:T(8,128)(2,1)S(1)}, u32[]{:S(2)}, u32[]{:S(2)}) async-start(bf16[64,8,512]{2,1,0:T(8,128)(2,1)} %bitcast.44), calls=%async_computation.3 | async-start | bytes 1048576 | tf_op jit(solution)/shard_map/all_to_all | solution.py:455
  79.4 11.7 %copy-start.1 = (f32[512,500]{0,1:T(8,128)S(1)}, f32[512,500]{0,1:T(8,128)}, u32[]{:S(2)}) copy-start(f32[512,500]{0,1:T(8,128)} %param.13) | copy-start | bytes 3072004
  79.8 6.0 %collective-permute-start = (bf16[504,128]{1,0:T(8,128)(2,1)S(1)}, bf16[504,128]{1,0:T(8,128)(2,1)S(1)}, u32[]{:S(2)}, u32[]{:S(2)}) collective-permute-start(bf16[504,128]{1,0:T(8,128)(2,1)S(1)} %get-tuple-element.49), channel_id=1, source_target_pairs={{0,64},{64,128},{128,192},{192,0},{1,65},{65,129},{129,193},{193,1... | collective-permute-start | bytes 387080 | tf_op jit(solution)/shard_map/ppermute | solution.py:460
  81.1 4.6 %collective-permute-start.2 = (bf16[504,128]{1,0:T(8,128)(2,1)S(1)}, bf16[504,128]{1,0:T(8,128)(2,1)S(1)}, u32[]{:S(2)}, u32[]{:S(2)}) collective-permute-start(bf16[504,128]{1,0:T(8,128)(2,1)S(1)} %get-tuple-element.50), channel_id=1, source_target_pairs={{0,192},{64,0},{128,64},{192,128},{1,193},{65,1},{129,65},{193,129... | collective-permute-start | bytes 387080 | tf_op jit(solution)/shard_map/ppermute | solution.py:460
  82.7 5.8 %collective-permute-start.4 = (bf16[504,128]{1,0:T(8,128)(2,1)S(1)}, bf16[504,128]{1,0:T(8,128)(2,1)S(1)}, u32[]{:S(2)}, u32[]{:S(2)}) collective-permute-start(bf16[504,128]{1,0:T(8,128)(2,1)S(1)} %get-tuple-element.51), channel_id=1, source_target_pairs={{0,64},{64,128},{128,192},{192,0},{1,65},{65,129},{129,193},{193,1... | collective-permute-start | bytes 387080 | tf_op jit(solution)/shard_map/ppermute | solution.py:460
  82.7 5.8 %collective-permute-start.5 = (bf16[504,128]{1,0:T(8,128)(2,1)S(1)}, bf16[504,128]{1,0:T(8,128)(2,1)S(1)}, u32[]{:S(2)}, u32[]{:S(2)}) collective-permute-start(bf16[504,128]{1,0:T(8,128)(2,1)S(1)} %get-tuple-element.52), channel_id=1, source_target_pairs={{0,192},{64,0},{128,64},{192,128},{1,193},{65,1},{129,65},{193,129... | collective-permute-start | bytes 387080 | tf_op jit(solution)/shard_map/ppermute | solution.py:460
  85.8 5.3 %collective-permute-start.1 = (bf16[504,128]{1,0:T(8,128)(2,1)S(1)}, bf16[504,128]{1,0:T(8,128)(2,1)S(1)}, u32[]{:S(2)}, u32[]{:S(2)}) collective-permute-start(bf16[504,128]{1,0:T(8,128)(2,1)S(1)} %collective-permute-done.before_low), channel_id=1, source_target_pairs={{0,64},{64,128},{128,192},{192,0},{1,65},{65,129},{129,193},{193,1... | collective-permute-start | bytes 387080 | tf_op jit(solution)/shard_map/ppermute | solution.py:460
  85.8 5.3 %collective-permute-start.3 = (bf16[504,128]{1,0:T(8,128)(2,1)S(1)}, bf16[504,128]{1,0:T(8,128)(2,1)S(1)}, u32[]{:S(2)}, u32[]{:S(2)}) collective-permute-start(bf16[504,128]{1,0:T(8,128)(2,1)S(1)} %collective-permute-done.2.after_high), channel_id=1, source_target_pairs={{0,192},{64,0},{128,64},{192,128},{1,193},{65,1},{129,65},{193,129... | collective-permute-start | bytes 387080 | tf_op jit(solution)/shard_map/ppermute | solution.py:460
  116.8 28.6 %copy-start.3 = (f32[500,512]{1,0:T(8,128)S(1)}, f32[500,512]{1,0:T(8,128)}, u32[]{:S(2)}) copy-start(f32[500,512]{1,0:T(8,128)} %copy-done.2) | copy-start | bytes 3072004
  136.2 6.5 %collective-permute-start.6 = (bf16[504,128]{1,0:T(8,128)(2,1)S(1)}, bf16[504,128]{1,0:T(8,128)(2,1)S(1)}, u32[]{:S(2)}, u32[]{:S(2)}) collective-permute-start(bf16[504,128]{1,0:T(8,128)(2,1)S(1)} %get-tuple-element.59), channel_id=1, source_target_pairs={{0,64},{64,128},{128,192},{192,0},{1,65},{65,129},{129,193},{193,1... | collective-permute-start | bytes 387080 | tf_op jit(solution)/shard_map/ppermute | solution.py:460
  137.5 5.2 %collective-permute-start.8 = (bf16[504,128]{1,0:T(8,128)(2,1)S(1)}, bf16[504,128]{1,0:T(8,128)(2,1)S(1)}, u32[]{:S(2)}, u32[]{:S(2)}) collective-permute-start(bf16[504,128]{1,0:T(8,128)(2,1)S(1)} %get-tuple-element.60), channel_id=1, source_target_pairs={{0,192},{64,0},{128,64},{192,128},{1,193},{65,1},{129,65},{193,129... | collective-permute-start | bytes 387080 | tf_op jit(solution)/shard_map/ppermute | solution.py:460
  139.4 10.8 %collective-permute-start.10 = (bf16[504,128]{1,0:T(8,128)(2,1)S(1)}, bf16[504,128]{1,0:T(8,128)(2,1)S(1)}, u32[]{:S(2)}, u32[]{:S(2)}) collective-permute-start(bf16[504,128]{1,0:T(8,128)(2,1)S(1)} %get-tuple-element.61), channel_id=1, source_target_pairs={{0,64},{64,128},{128,192},{192,0},{1,65},{65,129},{129,193},{193,1... | collective-permute-start | bytes 387080 | tf_op jit(solution)/shard_map/ppermute | solution.py:460
  139.4 10.8 %collective-permute-start.11 = (bf16[504,128]{1,0:T(8,128)(2,1)S(1)}, bf16[504,128]{1,0:T(8,128)(2,1)S(1)}, u32[]{:S(2)}, u32[]{:S(2)}) collective-permute-start(bf16[504,128]{1,0:T(8,128)(2,1)S(1)} %get-tuple-element.62), channel_id=1, source_target_pairs={{0,192},{64,0},{128,64},{192,128},{1,193},{65,1},{129,65},{193,129... | collective-permute-start | bytes 387080 | tf_op jit(solution)/shard_map/ppermute | solution.py:460
  142.7 8.0 %collective-permute-start.7 = (bf16[504,128]{1,0:T(8,128)(2,1)S(1)}, bf16[504,128]{1,0:T(8,128)(2,1)S(1)}, u32[]{:S(2)}, u32[]{:S(2)}) collective-permute-start(bf16[504,128]{1,0:T(8,128)(2,1)S(1)} %collective-permute-done.6.before_low), channel_id=1, source_target_pairs={{0,64},{64,128},{128,192},{192,0},{1,65},{65,129},{129,193},{193,1... | collective-permute-start | bytes 387080 | tf_op jit(solution)/shard_map/ppermute | solution.py:460
  142.7 8.0 %collective-permute-start.9 = (bf16[504,128]{1,0:T(8,128)(2,1)S(1)}, bf16[504,128]{1,0:T(8,128)(2,1)S(1)}, u32[]{:S(2)}, u32[]{:S(2)}) collective-permute-start(bf16[504,128]{1,0:T(8,128)(2,1)S(1)} %collective-permute-done.8.after_high), channel_id=1, source_target_pairs={{0,192},{64,0},{128,64},{192,128},{1,193},{65,1},{129,65},{193,129... | collective-permute-start | bytes 387080 | tf_op jit(solution)/shard_map/ppermute | solution.py:460
